TPU v7x, 256 devices: a whole 4x4x8 slice. The times are simulated.
256 devices in a mesh: gx: 32 (over z, y_hi, core), gz: 8 (over y_lo, x).
Axes of the slice: x: 4, y: 4 (y_hi: 2, y_lo: 2; y = y_hi * 2 + y_lo), z: 8, core: 2. Of those that a mesh axis runs over, the one named last changes fastest.
Arguments:
- density: float32 [4096, 8, 1024], P('gx', None, 'gz'), may hold values from 0.5 to 2
- momentum: float32 [3, 4096, 8, 1024], P(None, 'gx', None, 'gz'), may hold values from -3 to 3
- energy: float32 [4096, 8, 1024], P('gx', None, 'gz'), may hold values from 2 to 4
- costate: float32 [5, 4096, 8, 1024], P(None, 'gx', None, 'gz'), may hold values from -6 to 6
Outputs:
- adjoint: float32 [5, 4096, 8, 1024], P(None, 'gx', None, 'gz')
All inputs are finite; a program needn't handle non-finite values.
Results may differ from a plain program's by a relative error of at most 0.00005.
Values sent between devices are 32-bit elements; how exact they have to be, the bound alone decides.
No kernel may reach another device: no remote copies, remote signals or barrier semaphores. Data moves between devices by JAX's collectives and lax.ppermute only.
A program may use at most 128 MiB of HBM per device.

v0:
```python
import math

import jax
import jax.numpy as jnp
from jax import lax
from jax.sharding import PartitionSpec as P

pade_alpha = 1.0 / 3.0
near_coef = 14.0 / 9.0
far_coef = 1.0 / 9.0
step_scale = 0.1
gas_gamma = 1.4
highest = lax.Precision.HIGHEST


def fluxes(density, momentum, energy):
    inverse = 1.0 / density
    speed_stream = momentum[0] * inverse
    speed_span = momentum[2] * inverse
    kinetic = (
        0.5
        * (momentum[0] * momentum[0] + momentum[1] * momentum[1] + momentum[2] * momentum[2])
        * inverse
    )
    pressure = (gas_gamma - 1.0) * (energy - kinetic)
    enthalpy = energy + pressure
    flux_stream = jnp.stack(
        [
            momentum[0],
            momentum[0] * speed_stream + pressure,
            momentum[1] * speed_stream,
            momentum[2] * speed_stream,
            enthalpy * speed_stream,
        ]
    )
    flux_span = jnp.stack(
        [
            momentum[2],
            momentum[0] * speed_span,
            momentum[1] * speed_span,
            momentum[2] * speed_span + pressure,
            enthalpy * speed_span,
        ]
    )
    return (flux_stream, flux_span)


def green_matrix(length):
    pade_root = (-1.0 + math.sqrt(1.0 - 4.0 * pade_alpha * pade_alpha)) / (2.0 * pade_alpha)
    log_decay = math.log(-pade_root)
    row_index = lax.broadcasted_iota(jnp.int32, (length, length), 0) + 1
    col_index = lax.broadcasted_iota(jnp.int32, (length, length), 1) + 1

    def raised(exponent):
        parity = jnp.where(exponent % 2 == 0, 1.0, -1.0).astype(jnp.float32)
        return parity * jnp.exp(exponent.astype(jnp.float32) * log_decay)

    lesser = jnp.minimum(row_index, col_index)
    larger = jnp.maximum(row_index, col_index)
    scale_top = (1.0 - pade_root ** (2 * length + 2)) * pade_alpha * (pade_root - 1.0 / pade_root)
    return (
        raised(jnp.abs(row_index - col_index))
        * (1.0 - raised(2 * lesser))
        * (1.0 - raised(2 * (length + 1 - larger)))
        / scale_top
    )


def shaped(vector, line_axis, rank):
    layout = [1] * rank
    layout[line_axis] = vector.shape[0]
    return vector.reshape(layout)


def corrected(local_solve, prev_last, next_first, first_end, last_end, green_inv, line_axis):
    length = green_inv.shape[0]
    rank = local_solve.ndim
    coupling = pade_alpha * green_inv[0, 0]
    inv_det = 1.0 / (1.0 - coupling * coupling)
    left_value = (prev_last - coupling * first_end) * inv_det
    right_value = (next_first - coupling * last_end) * inv_det
    return local_solve - pade_alpha * (
        left_value * shaped(green_inv[:, 0], line_axis, rank)
        + right_value * shaped(green_inv[:, length - 1], line_axis, rank)
    )


def whole_lines(line_rows, green_inv):
    length = green_inv.shape[0]
    count, rows, cells = line_rows.shape
    blocks = cells // length
    stacked = line_rows.reshape(count, rows, blocks, length)
    local_solve = jnp.einsum("ij,fmbj->fmbi", green_inv, stacked, precision=highest)
    first_end = local_solve[..., 0:1]
    last_end = local_solve[..., length - 1 : length]
    solution = corrected(
        local_solve,
        jnp.roll(last_end, 1, axis=2),
        jnp.roll(first_end, -1, axis=2),
        first_end,
        last_end,
        green_inv,
        3,
    )
    solution = solution.reshape(count, rows, cells)
    return 0.5 * near_coef * (
        jnp.roll(solution, -1, axis=2) - jnp.roll(solution, 1, axis=2)
    ) + 0.25 * far_coef * (jnp.roll(solution, -2, axis=2) - jnp.roll(solution, 2, axis=2))


def derive_x(costate):
    fields, length, planes, span_cells = costate.shape
    green_inv = green_matrix(length)
    rows_last = jnp.moveaxis(costate, 1, 3).reshape(fields, planes * span_cells, length)

    def along_lines(line_rows):
        return whole_lines(line_rows, green_inv)

    slopes = along_lines(lax.all_to_all(rows_last, "gx", split_axis=1, concat_axis=2, tiled=True))
    returned = lax.all_to_all(slopes, "gx", split_axis=2, concat_axis=1, tiled=True)
    return jnp.moveaxis(returned.reshape(fields, planes, span_cells, length), 3, 1)


def derive_z(costate):
    fields, stream_cells, planes, length = costate.shape
    green_inv = green_matrix(length)
    rows_first = costate.reshape(fields, stream_cells * planes, length)

    def along_lines(line_rows):
        return whole_lines(line_rows, green_inv)

    slopes = along_lines(lax.all_to_all(rows_first, "gz", split_axis=1, concat_axis=2, tiled=True))
    returned = lax.all_to_all(slopes, "gz", split_axis=2, concat_axis=1, tiled=True)
    return returned.reshape(fields, stream_cells, planes, length)


def per_device(density, momentum, energy, costate):
    slope_stream = derive_x(costate)
    slope_span = derive_z(costate)
    primal_out, pullback_fn = jax.vjp(fluxes, density, momentum, energy)
    gradients = pullback_fn((slope_stream, slope_span))
    pulled = jnp.concatenate([gradients[0][None], gradients[1], gradients[2][None]], 0)
    return costate + step_scale * pulled


def solution(mesh):
    return jax.shard_map(
        per_device,
        mesh=mesh,
        in_specs=(
            P("gx", None, "gz"),
            P(None, "gx", None, "gz"),
            P("gx", None, "gz"),
            P(None, "gx", None, "gz"),
        ),
        out_specs=P(None, "gx", None, "gz"),
        check_vma=False,
    )
```

profile of v0, /device:TPU:8, one launch (start us, length us, event | category | flops | bytes accessed | tf_op | source)
XLA Modules:
  0.0 358.7 jit_solution(983776809151371864)
XLA Ops:
  0.0 5.3 %copy.142 = f32[5,128,8,128]{3,0,2,1:T(8,128)} copy(f32[5,128,8,128]{3,2,1,0:T(8,128)} %param.7) | data formatting | bytes 5242880 | tf_op args[3]
  5.3 7.0 %all-to-all-start = ((f32[5,1024,128]{2,0,1:T(8,128)}), f32[5,1024,128]{2,0,1:T(8,128)}, u32[]{:S(2)}, u32[]{:S(2)}) async-start(f32[5,1024,128]{2,0,1:T(8,128)} %bitcast.223), calls=%async_computation | async-start | bytes 8388608 | tf_op jit(solution)/shard_map/all_to_all | solution.py:132
  12.3 3.3 copy.155
  15.6 43.8 %all-to-all-done = f32[5,1024,128]{2,0,1:T(8,128)} async-done(((f32[5,1024,128]{2,0,1:T(8,128)}), f32[5,1024,128]{2,0,1:T(8,128)}, u32[]{:S(2)}, u32[]{:S(2)}) %all-to-all-start) | async-done | bytes 2621472 | tf_op jit(solution)/shard_map/all_to_all | solution.py:132
  59.4 11.2 %all-to-all-start.2 = ((f32[5,1024,128]{2,0,1:T(8,128)}), f32[5,1024,128]{2,0,1:T(8,128)}, u32[]{:S(2)}, u32[]{:S(2)}) async-start(f32[5,1024,128]{2,0,1:T(8,128)} %bitcast.222), calls=%async_computation.2 | async-start | bytes 8388608 | tf_op jit(solution)/shard_map/all_to_all | solution.py:119
  73.3 2.7 copy.143
  76.0 2.7 convolution_bitcast_fusion
  79.9 1.6 copy.177
  86.9 4.2 %fusion.1 = f32[5,128,1024]{1,0,2:T(8,128)} fusion(f32[5,128,1]{1,0,2:T(8,128)S(1)} %copy.178, f32[5,128,1023]{1,0,2:T(8,128)S(1)} %copy.177, f32[5,128,1023]{1,0,2:T(8,128)S(1)} %copy.180, f32[5,128,1]{1,0,2:T(8,128)S(1)} %copy.179, f32[5,128,2]{1,0,2:T(8,128)S(1)} %copy.182, f32[5,128,1022]{1,0,2:T(8,128)S(1)} %copy.181, f32[5,128,1022]{1,0,2:T(8,128)S(1)} %copy.184, ...), kind=kLoop, calls=%fused_computation.3 | loop fusion | flops 5898240 | bytes 13107200 | tf_op jit(solution)/shard_map/add | solution.py:106
  91.1 76.1 %all-to-all-done.2 = f32[5,1024,128]{2,0,1:T(8,128)} async-done(((f32[5,1024,128]{2,0,1:T(8,128)}), f32[5,1024,128]{2,0,1:T(8,128)}, u32[]{:S(2)}, u32[]{:S(2)}) %all-to-all-start.2) | async-done | bytes 2621472 | tf_op jit(solution)/shard_map/all_to_all | solution.py:119
  167.3 18.8 %all-to-all-start.1 = ((f32[5,128,1024]{1,0,2:T(8,128)}), f32[5,128,1024]{1,0,2:T(8,128)}, u32[]{:S(2)}, u32[]{:S(2)}) async-start(f32[5,128,1024]{1,0,2:T(8,128)} %fusion.1), calls=%async_computation.1 | async-start | bytes 8388608 | tf_op jit(solution)/shard_map/all_to_all | solution.py:133
  186.0 6.3 %fusion.7 = f32[128,5,32,32]{0,3,2,1:T(8,128)S(1)} fusion(f32[5,32,32,128]{3,0,2,1:T(8,128)} %bitcast.21, s32[128]{0:T(128)S(1)} %iota_add_fusion), kind=kOutput, calls=%fused_computation.13 | convolution fusion | flops 1007616000 | bytes 5243392 | tf_op jit(solution)/shard_map/ij,fmbj->fmbi/dot_general | solution.py:93
  192.4 9.0 %copy.159 = f32[128,5,32,32]{3,2,0,1:T(8,128)} copy(f32[128,5,32,32]{0,3,2,1:T(8,128)S(1)} %fusion.7) | data formatting | bytes 5242880 | tf_op jit(solution)/shard_map/ij,fmbj->fmbi/dot_general | solution.py:93
  204.5 10.0 %multiply_subtract_fusion = f32[5,32,32,128]{2,1,3,0:T(8,128)} fusion(f32[128]{0:T(128)S(1)} %get-tuple-element.58, f32[5,32,32]{2,1,0:T(8,128)S(1)} %get-tuple-element.13, f32[128]{0:T(128)S(1)} %get-tuple-element.57, f32[5,32,32]{2,1,0:T(8,128)S(1)} %get-tuple-element.12, f32[128,5,32,32]{3,2,0,1:T(8,128)} %copy.159), kind=kLoop, calls=%fused_computation | loop fusion | flops 3276800 | bytes 5284864 | tf_op jit(solution)/shard_map/sub | solution.py:82
  214.5 9.2 %copy.160 = f32[5,32,32,128]{3,2,1,0:T(8,128)} copy(f32[5,32,32,128]{2,1,3,0:T(8,128)} %multiply_subtract_fusion) | data formatting | bytes 5242880 | tf_op jit(solution)/shard_map/sub | solution.py:82
  223.6 2.6 reshape.45
  228.5 2.2 fusion.4
  230.7 8.8 %copy.161 = f32[5,32,4096]{1,0,2:T(8,128)} copy(f32[5,32,4096]{2,1,0:T(8,128)S(1)} %fusion.4) | data formatting | bytes 5242880 | tf_op jit(solution)/shard_map/add | solution.py:106
  239.5 12.7 %reshape.49 = f32[32,1,20480]{2,1,0:T(1,128)} reshape(f32[4096,5,32]{2,1,0:T(8,128)} %bitcast.209) | data formatting | bytes 5242880
  252.3 4.9 %all-to-all-start.3 = ((f32[32,1,20480]{2,1,0:T(1,128)}), f32[32,1,20480]{2,1,0:T(1,128)S(1)}, u32[]{:S(2)}, u32[]{:S(2)}) async-start(f32[32,1,20480]{2,1,0:T(1,128)} %reshape.49), calls=%async_computation.3 | async-start | bytes 5242880 | tf_op jit(solution)/shard_map/all_to_all | solution.py:120
  257.2 2.7 copy.153
  262.7 2.1 copy.166
  264.7 2.1 copy.154
  266.8 2.0 copy.165
  268.8 2.1 copy.168
  270.9 47.3 %all-to-all-done.3 = f32[32,1,20480]{2,1,0:T(1,128)S(1)} async-done(((f32[32,1,20480]{2,1,0:T(1,128)}), f32[32,1,20480]{2,1,0:T(1,128)S(1)}, u32[]{:S(2)}, u32[]{:S(2)}) %all-to-all-start.3) | async-done | bytes 2621472 | tf_op jit(solution)/shard_map/all_to_all | solution.py:120
  318.6 9.1 %reduce = f32[32,20480]{1,0:T(8,128)} reduce(f32[32,1,20480]{2,1,0:T(1,128)S(1)} %all-to-all-done.3, f32[]{:T(128)} %broadcast.157), dimensions={1}, to_apply=%all_to_all.53.reduce_sub_computation | reduce | bytes 5242884 | tf_op jit(solution)/shard_map/all_to_all | solution.py:120
  327.7 9.0 %reshape.50 = f32[4096,5,32]{2,1,0:T(8,128)} reshape(f32[32,20480]{1,0:T(8,128)} %reduce) | data formatting | bytes 5242880
  336.7 10.0 %copy.163 = f32[5,32,32,128]{3,2,1,0:T(8,128)} copy(f32[5,32,32,128]{2,0,3,1:T(8,128)} %bitcast.210) | data formatting | bytes 5242880 | tf_op jit(solution)/shard_map/all_to_all | solution.py:120
  346.7 2.6 copy.164
  349.3 3.0 fusion.22
  356.6 1.9 fusion.6
  (49 shorter events, 19.9 us)
Async XLA Ops:
  5.3 7.0 %copy-start = (f32[5,128,8,128]{3,2,1,0:T(8,128)S(1)}, f32[5,128,8,128]{3,2,1,0:T(8,128)}, u32[]{:S(2)}) copy-start(f32[5,128,8,128]{3,2,1,0:T(8,128)} %param.7) | copy-start | bytes 7864324
  5.3 54.1 %all-to-all-start = ((f32[5,1024,128]{2,0,1:T(8,128)}), f32[5,1024,128]{2,0,1:T(8,128)}, u32[]{:S(2)}, u32[]{:S(2)}) async-start(f32[5,1024,128]{2,0,1:T(8,128)} %bitcast.223), calls=%async_computation | async-start | bytes 8388608 | tf_op jit(solution)/shard_map/all_to_all | solution.py:132
  59.4 107.9 %all-to-all-start.2 = ((f32[5,1024,128]{2,0,1:T(8,128)}), f32[5,1024,128]{2,0,1:T(8,128)}, u32[]{:S(2)}, u32[]{:S(2)}) async-start(f32[5,1024,128]{2,0,1:T(8,128)} %bitcast.222), calls=%async_computation.2 | async-start | bytes 8388608 | tf_op jit(solution)/shard_map/all_to_all | solution.py:119
  167.3 85.0 %all-to-all-start.1 = ((f32[5,128,1024]{1,0,2:T(8,128)}), f32[5,128,1024]{1,0,2:T(8,128)}, u32[]{:S(2)}, u32[]{:S(2)}) async-start(f32[5,128,1024]{1,0,2:T(8,128)} %fusion.1), calls=%async_computation.1 | async-start | bytes 8388608 | tf_op jit(solution)/shard_map/all_to_all | solution.py:133
  252.3 65.9 %all-to-all-start.3 = ((f32[32,1,20480]{2,1,0:T(1,128)}), f32[32,1,20480]{2,1,0:T(1,128)S(1)}, u32[]{:S(2)}, u32[]{:S(2)}) async-start(f32[32,1,20480]{2,1,0:T(1,128)} %reshape.49), calls=%async_computation.3 | async-start | bytes 5242880 | tf_op jit(solution)/shard_map/all_to_all | solution.py:120
  349.3 3.0 copy-start.3
  349.3 3.0 copy-start.4
  352.3 1.4 copy-start.2
  352.3 1.5 copy-start.6
  353.8 1.0 copy-start.5
  353.8 1.0 copy-start.7
  354.9 1.7 copy-start.1
where the time goes:
time: 365 us; the launch traced here: 359 us
  waiting for transfers between devices  167 us (46%)
  local copies, waits for them, and re-layouts  105 us (29%)
  starting transfers between devices  41.8 us (11%)
  other arithmetic  33.5 us (9%)
  matrix products  9.03 us (2%)
    all_to_all x1, waiting for transfers between devices, derive_x(): lax.all_to_all(rows_last, 'gx', split_axis=1, concat_axis=2, tiled=True)  76.1 us
    all_to_all x1, waiting for transfers between devices, derive_x(): lax.all_to_all(slopes, 'gx', split_axis=2, concat_axis=1, tiled=True)  47.3 us
    all_to_all x1, waiting for transfers between devices, derive_z(): lax.all_to_all(rows_first, 'gz', split_axis=1, concat_axis=2, tiled=True)  43.8 us
    unnamed x27, local copies, waits for them, and re-layouts  36.7 us
    all_to_all x1, starting transfers between devices, derive_z(): lax.all_to_all(slopes, 'gz', split_axis=2, concat_axis=1, tiled=True)  18.8 us
    all_to_all x1, starting transfers between devices, derive_x(): lax.all_to_all(rows_last, 'gx', split_axis=1, concat_axis=2, tiled=True)  11.2 us
    another operation x6, local copies, waits for them, and re-layouts, fluxes(): jnp.stack([momentum[2], momentum[0] * speed_span, momentum[1] * speed_spa...  11 us
    sub x2, other arithmetic, corrected(): local_solve - pade_alpha * (left_value * shaped(green_inv[:, 0], line_axi...  10.6 us
  transfers between devices with their start and end apart: 4, of which 3 were waited for; matrix products, arithmetic and copies ran while one was open for 28% of the time, Pallas kernels for 0%

commit v1 on v0

v1 whole, which is shorter than its diff:
```python
import math

import jax
import jax.numpy as jnp
import ml_dtypes
import numpy as np
from jax import lax
from jax.experimental import pallas as pl
from jax.experimental.pallas import tpu as pltpu
from jax.sharding import PartitionSpec as P

pade_alpha = 1.0 / 3.0
near_coef = 14.0 / 9.0
far_coef = 1.0 / 9.0
step_scale = 0.1
gas_gamma = 1.4

root = (-1.0 + math.sqrt(1.0 - 4.0 * pade_alpha * pade_alpha)) / (2.0 * pade_alpha)
side = 0.25 * far_coef / pade_alpha
tail = (0.5 * near_coef - side) / pade_alpha

fields = 5
segments = 8
vmem_bytes = 48 * 1024 * 1024


def split(values):
    high = values.astype(ml_dtypes.bfloat16)
    low = (values - high.astype(np.float64)).astype(ml_dtypes.bfloat16)
    return high, low


def end_weights(length):
    cell = np.arange(length, dtype=np.float64)
    rows = np.zeros((4, length))
    rows[0] = root ** (length - cell)
    rows[1, length - 1] = 1.0
    rows[2] = root ** (cell + 1.0)
    rows[3, 0] = 1.0
    return rows


def stack_ends(rows):
    high, low = split(rows)
    stacked = np.zeros((16, rows.shape[1]), ml_dtypes.bfloat16)
    stacked[0:4] = high
    stacked[8:12] = low
    return stacked


def local_matrix(length):
    cell = np.arange(length)
    gap = cell[None, :] - cell[:, None]
    reach = np.abs(gap).astype(np.float64)
    taps = np.where(reach > 0, tail * root**reach, 0.0) - np.where(reach == 1, side, 0.0)
    high, low = split(np.sign(gap) * taps)
    return np.concatenate(
        [np.concatenate([high, low], 1), np.concatenate([high, low], 1)], 0
    )


def arrival_rows(length):
    cell = np.arange(length, dtype=np.float64)
    rows = np.zeros((4, length))
    rows[0] = tail * root**cell
    rows[1, 0] = -side
    rows[2] = -tail * root ** (length - 1.0 - cell)
    rows[3, length - 1] = side
    return rows


def stack_arrival(rows):
    high, low = split(rows)
    return np.concatenate([high, high, low, np.zeros_like(high)], 0)


def ends_kernel(rows, costate_hbm, weights_ref, even_x_ref, odd_x_ref, even_z_ref, odd_z_ref, held, sems):
    per_segment = rows // segments
    copies = [
        pltpu.make_async_copy(costate_hbm.at[c], held.at[c], sems.at[c]) for c in range(fields)
    ]
    for copy in copies:
        copy.start()
    x_even = lax.axis_index("gx") % 2 == 0
    z_even = lax.axis_index("gz") % 2 == 0
    weights = weights_ref[...]
    for c in range(fields):
        copies[c].wait()
        ahead = held[c, :, 0]
        back = held[c, :, per_segment - 1]
        for j in range(1, per_segment):
            ahead = ahead * root + held[c, :, j]
            back = back * root + held[c, :, per_segment - 1 - j]
        to_right = ahead[segments - 1] * root
        to_left = back[0] * root
        for s in range(1, segments):
            to_right = to_right + ahead[segments - 1 - s] * float(root ** (1 + s * per_segment))
            to_left = to_left + back[s] * float(root ** (1 + s * per_segment))
        first = held[c, 0, 0]
        last = held[c, segments - 1, per_segment - 1]
        even_x_ref[c, 0] = jnp.where(x_even, to_right, to_left)
        even_x_ref[c, 1] = jnp.where(x_even, last, first)
        odd_x_ref[c, 0] = jnp.where(x_even, to_left, to_right)
        odd_x_ref[c, 1] = jnp.where(x_even, first, last)
        lines = held[c].reshape(-1, 128)
        high = lines.astype(jnp.bfloat16)
        low = (lines - high.astype(jnp.float32)).astype(jnp.bfloat16)
        dims = (((1,), (1,)), ((), ()))
        sums = lax.dot_general(weights, high, dims, preferred_element_type=jnp.float32)
        sums = sums + lax.dot_general(weights, low, dims, preferred_element_type=jnp.float32)
        sums = sums[0:8] + sums[8:16]
        even_z_ref[c] = jnp.where(z_even, sums[0:2], sums[2:4])
        odd_z_ref[c] = jnp.where(z_even, sums[2:4], sums[0:2])


def pull(a, b, u0, u1, u2, h, k):
    a4u0 = a[4] * u0
    b4u2 = b[4] * u2
    both = a4u0 + b4u2
    g = (gas_gamma - 1.0) * (a[1] + b[3] + both)
    a1u0 = a[1] * u0
    b3u2 = b[3] * u2
    v0 = a1u0 + a[2] * u1 + a[3] * u2 + a[4] * h
    v2 = b[1] * u0 + b[2] * u1 + b3u2 + b[4] * h
    mass = g * k - v0 * u0 - v2 * u2
    m0 = a[0] + a1u0 + b[1] * u2 + v0 - g * u0
    m1 = a[2] * u0 + b[2] * u2 - g * u1
    m2 = b[0] + a[3] * u0 + b3u2 + v2 - g * u2
    energy = both + g
    return [mass, m0, m1, m2, energy]


def local_kernel(
    rows, density_ref, momentum_ref, energy_ref, costate_ref, matrix_ref, partial_ref, coef_ref, behind, span
):
    matrix = matrix_ref[...]
    for c in range(fields):
        lines = costate_ref[c].reshape(-1, 128)
        high = lines.astype(jnp.bfloat16)
        low = (lines - high.astype(jnp.float32)).astype(jnp.bfloat16)
        out = jnp.dot(
            jnp.concatenate([high, low], 1), matrix, preferred_element_type=jnp.float32
        )
        span[c] = (out[:, :128] + out[:, 128:]).reshape(rows, 8, 128)

    def backward(step, carry):
        i = rows - 1 - step
        nxt = []
        for c in range(fields):
            behind[c, i] = carry[c]
            nxt.append(carry[c] * root + costate_ref[c, i] * (tail * root))
        return tuple(nxt)

    zero = jnp.zeros((8, 128), jnp.float32)
    lax.fori_loop(0, rows, backward, (zero,) * fields, unroll=8)

    def forward(i, carry):
        ahead, before, now = carry
        upper = jnp.minimum(i + 1, rows - 1)
        more = jnp.where(i + 1 < rows, 1.0, 0.0).astype(jnp.float32)
        inverse = 1.0 / density_ref[i]
        u0 = momentum_ref[0, i] * inverse
        u1 = momentum_ref[1, i] * inverse
        u2 = momentum_ref[2, i] * inverse
        k = 0.5 * (u0 * u0 + u1 * u1 + u2 * u2)
        h = gas_gamma * (energy_ref[i] * inverse) - (gas_gamma - 1.0) * k
        after = [costate_ref[c, upper] * more for c in range(fields)]
        a = [
            (ahead[c] - behind[c, i]) + side * (after[c] - before[c]) for c in range(fields)
        ]
        b = [span[c, i] for c in range(fields)]
        pulled = pull(a, b, u0, u1, u2, h, k)
        for c in range(fields):
            partial_ref[c, i] = now[c] + step_scale * pulled[c]
        for slot, value in enumerate((u0, u1, u2, h, k)):
            coef_ref[slot, i] = value
        ahead = tuple(ahead[c] * root + now[c] * (tail * root) for c in range(fields))
        return ahead, now, tuple(after)

    start = tuple(costate_ref[c, 0] for c in range(fields))
    lax.fori_loop(0, rows, forward, ((zero,) * fields, (zero,) * fields, start), unroll=4)


def join_kernel(
    rows, partial_ref, coef_ref, even_x_ref, odd_x_ref, even_z_ref, odd_z_ref, arrive_ref, scale_ref, out_ref, span
):
    x_even = lax.axis_index("gx") % 2 == 0
    z_even = lax.axis_index("gz") % 2 == 0
    arrive = arrive_ref[...]
    for c in range(fields):
        even = even_z_ref[c]
        odd = odd_z_ref[c]
        values = jnp.concatenate(
            [jnp.where(z_even, odd, even), jnp.where(z_even, even, odd)], 0
        )
        high = values.astype(jnp.bfloat16).astype(jnp.float32)
        low = values - high
        stacked = jnp.concatenate([high, low, high, jnp.zeros_like(high)], 0)
        columns = jnp.swapaxes(stacked, 0, 1).astype(jnp.bfloat16)
        span[c] = jnp.dot(columns, arrive, preferred_element_type=jnp.float32).reshape(rows, 8, 128)
    left_sum = [jnp.where(x_even, odd_x_ref[c, 0], even_x_ref[c, 0]) for c in range(fields)]
    right_sum = [jnp.where(x_even, even_x_ref[c, 0], odd_x_ref[c, 0]) for c in range(fields)]

    def add(i, a):
        u0, u1, u2, h, k = [coef_ref[slot, i] for slot in range(5)]
        b = [span[c, i] for c in range(fields)]
        pulled = pull(a, b, u0, u1, u2, h, k)
        for c in range(fields):
            out_ref[c, i] = partial_ref[c, i] + step_scale * pulled[c]

    def stream(i):
        return [left_sum[c] * scale_ref[0, i] + right_sum[c] * scale_ref[1, i] for c in range(fields)]

    def body(i, carry):
        add(i, stream(i))
        return carry

    first = stream(0)
    last = stream(rows - 1)
    for c in range(fields):
        left_edge = jnp.where(x_even, odd_x_ref[c, 1], even_x_ref[c, 1])
        right_edge = jnp.where(x_even, even_x_ref[c, 1], odd_x_ref[c, 1])
        first[c] = first[c] - side * left_edge
        last[c] = last[c] + side * right_edge
    add(0, first)
    lax.fori_loop(1, rows - 1, body, 0, unroll=3)
    add(rows - 1, last)


def per_device(density, momentum, energy, costate):
    rows, planes, cells = density.shape
    f32 = jnp.float32
    whole = pl.BlockSpec(memory_space=pltpu.VMEM)
    params = pltpu.CompilerParams(vmem_limit_bytes=vmem_bytes)
    x_shape = jax.ShapeDtypeStruct((fields, 2, planes, cells), f32)
    z_shape = jax.ShapeDtypeStruct((fields, 2, rows * planes), f32)
    block = jax.ShapeDtypeStruct((fields, rows, planes, cells), f32)
    per_segment = rows // segments

    even_x, odd_x, even_z, odd_z = pl.pallas_call(
        lambda *refs: ends_kernel(rows, *refs),
        out_shape=(x_shape, x_shape, z_shape, z_shape),
        in_specs=[pl.BlockSpec(memory_space=pl.ANY), whole],
        out_specs=(whole,) * 4,
        scratch_shapes=[
            pltpu.VMEM((fields, segments, per_segment, planes, cells), f32),
            pltpu.SemaphoreType.DMA((fields,)),
        ],
        compiler_params=params,
        name="ends",
    )(
        costate.reshape(fields, segments, per_segment, planes, cells),
        jnp.asarray(stack_ends(end_weights(cells))),
    )

    def pairs(values, axis, odd):
        count = lax.axis_size(axis)
        links = []
        for i in range(odd, count + odd, 2):
            a, b = i % count, (i + 1) % count
            links += [(a, b), (b, a)]
        return lax.ppermute(values, axis, links)

    even_x = pairs(even_x, "gx", 0)
    even_z = pairs(even_z, "gz", 0)
    odd_z = pairs(odd_z, "gz", 1)
    odd_x = pairs(odd_x, "gx", 1)

    partial, coef = pl.pallas_call(
        lambda *refs: local_kernel(rows, *refs),
        out_shape=(block, block),
        in_specs=[whole] * 5,
        out_specs=(whole,) * 2,
        scratch_shapes=[
            pltpu.VMEM((fields, rows, planes, cells), f32),
            pltpu.VMEM((fields, rows, planes, cells), f32),
        ],
        compiler_params=params,
        cost_estimate=pl.CostEstimate(flops=300_000_000, bytes_accessed=10_000_000, transcendentals=0),
        name="local",
    )(density, momentum, energy, costate, jnp.asarray(local_matrix(cells)))

    rows_x = arrival_rows(rows)
    scale = jnp.asarray(rows_x[0::2].astype(np.float32))
    return pl.pallas_call(
        lambda *refs: join_kernel(rows, *refs),
        out_shape=block,
        in_specs=[whole] * 7 + [pl.BlockSpec(memory_space=pltpu.SMEM)],
        out_specs=whole,
        scratch_shapes=[pltpu.VMEM((fields, rows, planes, cells), f32)],
        compiler_params=params,
        name="join",
    )(
        partial,
        coef,
        even_x,
        odd_x,
        even_z,
        odd_z,
        jnp.asarray(stack_arrival(arrival_rows(cells))),
        scale,
    )


def solution(mesh):
    return jax.shard_map(
        per_device,
        mesh=mesh,
        in_specs=(
            P("gx", None, "gz"),
            P(None, "gx", None, "gz"),
            P("gx", None, "gz"),
            P(None, "gx", None, "gz"),
        ),
        out_specs=P(None, "gx", None, "gz"),
        check_vma=False,
    )
```

time: 365 us -> 30.5 us (0.08); the launches traced: 359 us -> 30.2 us
  waiting for transfers between devices: 167 us -> 0.01 us
  local copies, waits for them, and re-layouts: 105 us -> 5.08 us
  other arithmetic: 33.5 us -> 0 us
  starting transfers between devices: 41.8 us -> 12.2 us
  Pallas kernels: 0 us -> 12.9 us
  matrix products: 9.03 us -> 0 us
    all_to_all x4 -> x0, waiting for transfers between devices: 167 us -> none  [the longest x1 76.1 us: derive_x(): lax.all_to_all(rows_last, 'gx', split_axis=1, concat_axis=2, tiled=True)]
    all_to_all x4 -> x0, starting transfers between devices: 41.8 us -> none  [the longest x1 18.8 us: derive_z(): lax.all_to_all(slopes, 'gz', split_axis=2, concat_axis=1, tiled=True)]
    unnamed x27 -> x18, local copies, waits for them, and re-layouts: 36.7 us -> 5.08 us
    all_to_all x4 -> x0, local copies, waits for them, and re-layouts: 15.9 us -> none  [the longest x2 10.5 us: derive_x(): lax.all_to_all(slopes, 'gx', split_axis=2, concat_axis=1, tiled=True)]
    pallas_call x0 -> x3, Pallas kernels: none -> 12.9 us  [the longest x1 6.81 us: per_device(): pl.pallas_call(lambda *refs: local_kernel(rows, *refs), out_shape=(block,...]
    ppermute x0 -> x4, starting transfers between devices: none -> 12.2 us  [pairs(): return lax.ppermute(values, axis, links)]
    another operation x6 -> x0, local copies, waits for them, and re-layouts: 11 us -> none  [fluxes(): jnp.stack([momentum[2], momentum[0] * speed_span, momentum[1] * speed_spa...]
    sub x2 -> x0, other arithmetic: 10.6 us -> none  [corrected(): local_solve - pade_alpha * (left_value * shaped(green_inv[:, 0], line_axi...]
  transfers between devices with their start and end apart: 4 -> 4, of which waited for: 3 -> 0; matrix products, arithmetic and copies ran while one was open for 28% -> 0% of each run, Pallas kernels for 0% -> 23%
where the time goes in v1:
time: 30.5 us; the launch traced here: 30.2 us
  Pallas kernels  12.9 us (42%)
  starting transfers between devices  12.2 us (40%)
  local copies, waits for them, and re-layouts  5.08 us (17%)
    ppermute x4, starting transfers between devices, pairs(): return lax.ppermute(values, axis, links)  12.2 us
    pallas_call x1, Pallas kernels, per_device(): pl.pallas_call(lambda *refs: local_kernel(rows, *refs), out_shape=(block,...  6.81 us
    unnamed x18, local copies, waits for them, and re-layouts  5.08 us
    pallas_call x1, Pallas kernels, per_device(): pl.pallas_call(lambda *refs: join_kernel(rows, *refs), out_shape=block, i...  4.2 us
    pallas_call x1, Pallas kernels, per_device(): pl.pallas_call(lambda *refs: ends_kernel(rows, *refs), out_shape=(x_shape...  1.92 us
  transfers between devices with their start and end apart: 4, of which 0 were waited for; matrix products, arithmetic and copies ran while one was open for 0% of the time, Pallas kernels for 23%

profile of v1, /device:TPU:8, one launch (start us, length us, event | category | flops | bytes accessed | tf_op | source)
XLA Modules:
  0.0 30.2 jit_solution(6397500695778298616)
XLA Ops:
  0.0 0.0 copy-start
  0.0 1.7 %copy-done = f32[5,128,8,128]{3,2,1,0:T(8,128)S(1)} copy-done((f32[5,128,8,128]{3,2,1,0:T(8,128)S(1)}, f32[5,128,8,128]{3,2,1,0:T(8,128)}, u32[]{:S(2)}) %copy-start) | copy-done | bytes 2621464
  1.7 0.0 copy-start.7
  1.7 0.7 %copy-done.7 = bf16[16,128]{1,0:T(8,128)(2,1)S(1)} copy-done((bf16[16,128]{1,0:T(8,128)(2,1)S(1)}, bf16[16,128]{1,0:T(8,128)(2,1)}, u32[]{:S(2)}) %copy-start.7) | copy-done | bytes 4120
  2.4 0.0 copy-start.2
  2.4 0.0 copy-start.3
  2.4 0.0 copy-start.4
  2.4 1.9 %ends.1 = (f32[5,2,8,128]{3,2,1,0:T(8,128)S(1)}, f32[5,2,8,128]{3,2,1,0:T(8,128)S(1)}, f32[5,2,1024]{2,1,0:T(2,128)S(1)}, f32[5,2,1024]{2,1,0:T(2,128)S(1)}) custom-call(f32[5,8,16,8,128]{4,3,2,1,0:T(8,128)S(1)} %bitcast.1, bf16[16,128]{1,0:T(8,128)(2,1)S(1)} %copy-done.7), custom_call_target="tpu_custom_call" | custom-call | tf_op jit(solution)/shard_map/ends/pallas_call | solution.py:240
  4.4 0.1 collective-permute-start
  4.5 7.7 %collective-permute-start.1 = (f32[5,2,8,128]{3,2,1,0:T(8,128)S(1)}, f32[5,2,8,128]{3,2,1,0:T(8,128)S(1)}, u32[]{:S(2)}, u32[]{:S(2)}) collective-permute-start(f32[5,2,8,128]{3,2,1,0:T(8,128)S(1)} %get-tuple-element.14), channel_id=1, source_target_pairs={{8,16},{16,8},{24,32},{32,24},{40,48},{48,40},{56,64},{64,56},{72,... | collective-permute-start | bytes 122888 | tf_op jit(solution)/shard_map/ppermute | solution.py:262
  12.2 1.5 %collective-permute-start.2 = (f32[5,2,1024]{2,1,0:T(2,128)S(1)}, f32[5,2,1024]{2,1,0:T(2,128)S(1)}, u32[]{:S(2)}, u32[]{:S(2)}) collective-permute-start(f32[5,2,1024]{2,1,0:T(2,128)S(1)} %get-tuple-element.15), channel_id=1, source_target_pairs={{0,1},{1,0},{2,3},{3,2},{4,5},{5,4},{6,7},{7,6},{8,9},{9,8},{10,11... | collective-permute-start | bytes 122888 | tf_op jit(solution)/shard_map/ppermute | solution.py:262
  13.6 2.9 %collective-permute-start.3 = (f32[5,2,1024]{2,1,0:T(2,128)S(1)}, f32[5,2,1024]{2,1,0:T(2,128)S(1)}, u32[]{:S(2)}, u32[]{:S(2)}) collective-permute-start(f32[5,2,1024]{2,1,0:T(2,128)S(1)} %get-tuple-element.16), channel_id=1, source_target_pairs={{1,2},{2,1},{3,4},{4,3},{5,6},{6,5},{7,0},{0,7},{9,10},{10,9},{11,... | collective-permute-start | bytes 122888 | tf_op jit(solution)/shard_map/ppermute | solution.py:262
  16.5 0.0 copy-done.2
  16.5 0.0 copy-done.3
  16.5 0.0 copy-done.4
  16.5 0.0 copy-start.5
  16.5 0.9 %copy-done.5 = bf16[256,256]{1,0:T(8,128)(2,1)S(1)} copy-done((bf16[256,256]{1,0:T(8,128)(2,1)S(1)}, bf16[256,256]{1,0:T(8,128)(2,1)}, u32[]{:S(2)}) %copy-start.5) | copy-done | bytes 131096
  17.4 0.0 copy-start.6
  17.4 0.0 copy-start.8
  17.4 6.8 %local.1 = (f32[5,128,8,128]{3,2,1,0:T(8,128)S(1)}, f32[5,128,8,128]{3,2,1,0:T(8,128)}) custom-call(f32[128,8,128]{2,1,0:T(8,128)S(1)} %copy-done.3, f32[3,128,8,128]{3,2,1,0:T(8,128)S(1)} %copy-done.2, f32[128,8,128]{2,1,0:T(8,128)S(1)} %copy-done.4, f32[5,128,8,128]{3,2,1,0:T(8,128)} %refs_3_.1, bf16[256,256]{1,0:T(8,128)(2,1)S(1)} %copy-done.5), custom_call_target="tpu_custom_call" | custom-call | flops 300000000 | bytes 10000000 | tf_op jit(solution)/shard_map/local/pallas_call | solution.py:269
  24.2 0.0 collective-permute-done.refs_2_
  24.3 0.0 collective-permute-done.1.refs_3_
  24.3 0.0 collective-permute-done.2.refs_4_
  24.3 0.0 collective-permute-done.3.refs_5_
  24.3 0.0 copy-done.6
  24.3 0.0 copy-done.8
  24.3 0.0 copy-start.1
  24.3 1.7 %copy-done.1 = f32[5,128,8,128]{3,2,1,0:T(8,128)S(1)} copy-done((f32[5,128,8,128]{3,2,1,0:T(8,128)S(1)}, f32[5,128,8,128]{3,2,1,0:T(8,128)}, u32[]{:S(2)}) %copy-start.1) | copy-done | bytes 2621464
  26.0 4.2 %join.1 = f32[5,128,8,128]{3,2,1,0:T(8,128)} custom-call(f32[5,128,8,128]{3,2,1,0:T(8,128)S(1)} %get-tuple-element.11.refs_0_, f32[5,128,8,128]{3,2,1,0:T(8,128)S(1)} %copy-done.1, f32[5,2,8,128]{3,2,1,0:T(8,128)S(1)} %collective-permute-done.refs_2_, f32[5,2,8,128]{3,2,1,0:T(8,128)S(1)} %collective-permute-done.1.refs_3_, ...), custom_call_target="tpu_custom_call" | custom-call | tf_op jit(solution)/shard_map/join/pallas_call | solution.py:285
Async XLA Ops:
  0.0 1.7 %copy-start = (f32[5,128,8,128]{3,2,1,0:T(8,128)S(1)}, f32[5,128,8,128]{3,2,1,0:T(8,128)}, u32[]{:S(2)}) copy-start(f32[5,128,8,128]{3,2,1,0:T(8,128)} %refs_3_.1) | copy-start | bytes 7864324
  1.7 0.7 %copy-start.7 = (bf16[16,128]{1,0:T(8,128)(2,1)S(1)}, bf16[16,128]{1,0:T(8,128)(2,1)}, u32[]{:S(2)}) copy-start(bf16[16,128]{1,0:T(8,128)(2,1)} %constant.8.clone.refs_1_) | copy-start | bytes 12292
  2.4 14.1 %copy-start.2 = (f32[3,128,8,128]{3,2,1,0:T(8,128)S(1)}, f32[3,128,8,128]{3,2,1,0:T(8,128)}, u32[]{:S(2)}) copy-start(f32[3,128,8,128]{3,2,1,0:T(8,128)} %refs_1_.2) | copy-start | bytes 4718596
  2.4 14.1 %copy-start.3 = (f32[128,8,128]{2,1,0:T(8,128)S(1)}, f32[128,8,128]{2,1,0:T(8,128)}, u32[]{:S(2)}) copy-start(f32[128,8,128]{2,1,0:T(8,128)} %refs_0_.1) | copy-start | bytes 1572868
  2.4 14.1 %copy-start.4 = (f32[128,8,128]{2,1,0:T(8,128)S(1)}, f32[128,8,128]{2,1,0:T(8,128)}, u32[]{:S(2)}) copy-start(f32[128,8,128]{2,1,0:T(8,128)} %refs_2_.1) | copy-start | bytes 1572868
  4.4 19.9 %collective-permute-start = (f32[5,2,8,128]{3,2,1,0:T(8,128)S(1)}, f32[5,2,8,128]{3,2,1,0:T(8,128)S(1)}, u32[]{:S(2)}, u32[]{:S(2)}) collective-permute-start(f32[5,2,8,128]{3,2,1,0:T(8,128)S(1)} %get-tuple-element.13), channel_id=1, source_target_pairs={{0,8},{8,0},{16,24},{24,16},{32,40},{40,32},{48,56},{56,48},{64,72... | collective-permute-start | bytes 122888 | tf_op jit(solution)/shard_map/ppermute | solution.py:262
  4.5 19.8 %collective-permute-start.1 = (f32[5,2,8,128]{3,2,1,0:T(8,128)S(1)}, f32[5,2,8,128]{3,2,1,0:T(8,128)S(1)}, u32[]{:S(2)}, u32[]{:S(2)}) collective-permute-start(f32[5,2,8,128]{3,2,1,0:T(8,128)S(1)} %get-tuple-element.14), channel_id=1, source_target_pairs={{8,16},{16,8},{24,32},{32,24},{40,48},{48,40},{56,64},{64,56},{72,... | collective-permute-start | bytes 122888 | tf_op jit(solution)/shard_map/ppermute | solution.py:262
  12.2 12.1 %collective-permute-start.2 = (f32[5,2,1024]{2,1,0:T(2,128)S(1)}, f32[5,2,1024]{2,1,0:T(2,128)S(1)}, u32[]{:S(2)}, u32[]{:S(2)}) collective-permute-start(f32[5,2,1024]{2,1,0:T(2,128)S(1)} %get-tuple-element.15), channel_id=1, source_target_pairs={{0,1},{1,0},{2,3},{3,2},{4,5},{5,4},{6,7},{7,6},{8,9},{9,8},{10,11... | collective-permute-start | bytes 122888 | tf_op jit(solution)/shard_map/ppermute | solution.py:262
  13.6 10.6 %collective-permute-start.3 = (f32[5,2,1024]{2,1,0:T(2,128)S(1)}, f32[5,2,1024]{2,1,0:T(2,128)S(1)}, u32[]{:S(2)}, u32[]{:S(2)}) collective-permute-start(f32[5,2,1024]{2,1,0:T(2,128)S(1)} %get-tuple-element.16), channel_id=1, source_target_pairs={{1,2},{2,1},{3,4},{4,3},{5,6},{6,5},{7,0},{0,7},{9,10},{10,9},{11,... | collective-permute-start | bytes 122888 | tf_op jit(solution)/shard_map/ppermute | solution.py:262
  16.5 0.9 %copy-start.5 = (bf16[256,256]{1,0:T(8,128)(2,1)S(1)}, bf16[256,256]{1,0:T(8,128)(2,1)}, u32[]{:S(2)}) copy-start(bf16[256,256]{1,0:T(8,128)(2,1)} %constant.9.clone.refs_4_) | copy-start | bytes 393220
  17.4 6.8 %copy-start.6 = (bf16[16,128]{1,0:T(8,128)(2,1)S(1)}, bf16[16,128]{1,0:T(8,128)(2,1)}, u32[]{:S(2)}) copy-start(bf16[16,128]{1,0:T(8,128)(2,1)} %constant.11.clone.refs_6_) | copy-start | bytes 12292
  17.4 6.8 %copy-start.8 = (f32[2,128]{1,0:T(2,128)S(1)}, f32[2,128]{1,0:T(2,128)}, u32[]{:S(2)}) copy-start(f32[2,128]{1,0:T(2,128)} %constant.10.clone.refs_7_) | copy-start | bytes 3076
  24.3 1.7 %copy-start.1 = (f32[5,128,8,128]{3,2,1,0:T(8,128)S(1)}, f32[5,128,8,128]{3,2,1,0:T(8,128)}, u32[]{:S(2)}) copy-start(f32[5,128,8,128]{3,2,1,0:T(8,128)} %get-tuple-element.12.refs_1_) | copy-start | bytes 7864324

commit v2 on v1

v2 whole, which is shorter than its diff:
```python
import math

import jax
import jax.numpy as jnp
import ml_dtypes
import numpy as np
from jax import lax
from jax.experimental import pallas as pl
from jax.experimental.pallas import tpu as pltpu
from jax.sharding import PartitionSpec as P

pade_alpha = 1.0 / 3.0
near_coef = 14.0 / 9.0
far_coef = 1.0 / 9.0
step_scale = 0.1
gas_gamma = 1.4

root = (-1.0 + math.sqrt(1.0 - 4.0 * pade_alpha * pade_alpha)) / (2.0 * pade_alpha)
side = 0.25 * far_coef / pade_alpha
tail = (0.5 * near_coef - side) / pade_alpha

fields = 5
segments = 8
vmem_bytes = 16 * 1024 * 1024


def split(values):
    high = values.astype(ml_dtypes.bfloat16)
    low = (values - high.astype(np.float64)).astype(ml_dtypes.bfloat16)
    return high, low


def end_weights(length):
    cell = np.arange(length, dtype=np.float64)
    rows = np.zeros((4, length))
    rows[0] = root ** (length - cell)
    rows[1, length - 1] = 1.0
    rows[2] = root ** (cell + 1.0)
    rows[3, 0] = 1.0
    return rows


def stack_ends(rows):
    high, low = split(rows)
    stacked = np.zeros((16, rows.shape[1]), ml_dtypes.bfloat16)
    stacked[0:4] = high
    stacked[8:12] = low
    return stacked


def local_matrix(length):
    cell = np.arange(length)
    gap = cell[None, :] - cell[:, None]
    reach = np.abs(gap).astype(np.float64)
    taps = np.where(reach > 0, tail * root**reach, 0.0) - np.where(reach == 1, side, 0.0)
    high, low = split(step_scale * np.sign(gap) * taps)
    return np.concatenate(
        [np.concatenate([high, low], 1), np.concatenate([high, low], 1)], 0
    )


def arrival_rows(length):
    cell = np.arange(length, dtype=np.float64)
    rows = np.zeros((4, length))
    rows[0] = tail * root**cell
    rows[1, 0] = -side
    rows[2] = -tail * root ** (length - 1.0 - cell)
    rows[3, length - 1] = side
    return rows


def stack_arrival(rows):
    high, low = split(rows)
    return np.concatenate([high, high, low, np.zeros_like(high)], 0)


def in_hbm(values):
    return pltpu.with_memory_space_constraint(values, pltpu.HBM)


def ends_kernel(
    rows, costate_hbm, weights_hbm, held, even_x_ref, even_z_ref, odd_z_ref, odd_x_ref, weights_ref, sems
):
    per_segment = rows // segments
    weights_copy = pltpu.make_async_copy(weights_hbm, weights_ref, sems.at[fields])
    copies = [
        pltpu.make_async_copy(costate_hbm.at[c], held.at[c], sems.at[c]) for c in range(fields)
    ]
    weights_copy.start()
    for copy in copies:
        copy.start()
    x_even = lax.axis_index("gx") % 2 == 0
    z_even = lax.axis_index("gz") % 2 == 0
    weights_copy.wait()

    def component(c, carry):
        pltpu.make_async_copy(costate_hbm.at[c], held.at[c], sems.at[c]).wait()
        weights = weights_ref[...]
        ahead = held[c, :, 0]
        back = held[c, :, per_segment - 1]
        for j in range(1, per_segment):
            ahead = ahead * root + held[c, :, j]
            back = back * root + held[c, :, per_segment - 1 - j]
        to_right = ahead[segments - 1] * root
        to_left = back[0] * root
        for s in range(1, segments):
            to_right = to_right + ahead[segments - 1 - s] * float(root ** (1 + s * per_segment))
            to_left = to_left + back[s] * float(root ** (1 + s * per_segment))
        first = held[c, 0, 0]
        last = held[c, segments - 1, per_segment - 1]
        even_x_ref[c, 0] = jnp.where(x_even, to_right, to_left)
        even_x_ref[c, 1] = jnp.where(x_even, last, first)
        odd_x_ref[c, 0] = jnp.where(x_even, to_left, to_right)
        odd_x_ref[c, 1] = jnp.where(x_even, first, last)
        lines = held[c].reshape(-1, 128)
        high = lines.astype(jnp.bfloat16)
        low = (lines - high.astype(jnp.float32)).astype(jnp.bfloat16)
        dims = (((1,), (1,)), ((), ()))
        sums = lax.dot_general(weights, high, dims, preferred_element_type=jnp.float32)
        sums = sums + lax.dot_general(weights, low, dims, preferred_element_type=jnp.float32)
        sums = sums[0:8] + sums[8:16]
        even_z_ref[c] = jnp.where(z_even, sums[0:2], sums[2:4])
        odd_z_ref[c] = jnp.where(z_even, sums[2:4], sums[0:2])
        return carry

    lax.fori_loop(0, fields, component, 0)


def pull(a, b, u0, u1, u2, h, k):
    a4u0 = a[4] * u0
    b4u2 = b[4] * u2
    both = a4u0 + b4u2
    g = (gas_gamma - 1.0) * (a[1] + b[3] + both)
    a1u0 = a[1] * u0
    b3u2 = b[3] * u2
    v0 = a1u0 + a[2] * u1 + a[3] * u2 + a[4] * h
    v2 = b[1] * u0 + b[2] * u1 + b3u2 + b[4] * h
    mass = g * k - v0 * u0 - v2 * u2
    m0 = a[0] + a1u0 + b[1] * u2 + v0 - g * u0
    m1 = a[2] * u0 + b[2] * u2 - g * u1
    m2 = b[0] + a[3] * u0 + b3u2 + v2 - g * u2
    energy = both + g
    return [mass, m0, m1, m2, energy]


def local_kernel(
    rows, costate_ref, matrix_hbm, density_hbm, momentum_hbm, energy_hbm, partial_ref, coef_ref,
    behind, span, matrix_ref, density_ref, momentum_ref, energy_ref, sems,
):
    copies = [
        pltpu.make_async_copy(source, target, sems.at[n])
        for n, (source, target) in enumerate(
            (
                (matrix_hbm, matrix_ref),
                (density_hbm, density_ref),
                (momentum_hbm, momentum_ref),
                (energy_hbm, energy_ref),
            )
        )
    ]
    for copy in copies:
        copy.start()
    zero = jnp.zeros((8, 128), jnp.float32)
    gain = step_scale * tail
    edge = step_scale * side
    for c in range(fields):
        behind[c, rows - 1] = zero
    zero = behind[0, rows - 1]

    def backward(step, carry):
        i = rows - 2 - step
        nxt = []
        for c in range(fields):
            after = costate_ref[c, i + 1]
            now = carry[c] * root + after * (gain * root)
            behind[c, i] = now - after * edge
            nxt.append(now)
        return tuple(nxt)

    lax.fori_loop(0, rows - 1, backward, (zero,) * fields, unroll=8)
    copies[0].wait()

    def across(c, carry):
        lines = costate_ref[c].reshape(-1, 128)
        high = lines.astype(jnp.bfloat16)
        low = (lines - high.astype(jnp.float32)).astype(jnp.bfloat16)
        out = jnp.dot(
            jnp.concatenate([high, low], 1), matrix_ref[...], preferred_element_type=jnp.float32
        )
        span[c] = (out[:, :128] + out[:, 128:]).reshape(rows, 8, 128)
        return carry

    lax.fori_loop(0, fields, across, 0)
    for copy in copies[1:]:
        copy.wait()

    def forward(i, carry):
        ahead, before = carry
        rho = density_ref[i]
        inverse = pl.reciprocal(rho, approx=True)
        inverse = inverse * (2.0 - rho * inverse)
        inverse = inverse * (2.0 - rho * inverse)
        u0 = momentum_ref[0, i] * inverse
        u1 = momentum_ref[1, i] * inverse
        u2 = momentum_ref[2, i] * inverse
        k = 0.5 * (u0 * u0 + u1 * u1 + u2 * u2)
        h = gas_gamma * (energy_ref[i] * inverse) - (gas_gamma - 1.0) * k
        ahead = tuple(ahead[c] * root + before[c] * (gain * root) for c in range(fields))
        a = [ahead[c] - before[c] * edge - behind[c, i] for c in range(fields)]
        b = [span[c, i] for c in range(fields)]
        pulled = pull(a, b, u0, u1, u2, h, k)
        now = tuple(costate_ref[c, i] for c in range(fields))
        for c in range(fields):
            partial_ref[c, i] = now[c] + pulled[c]
        for slot, value in enumerate((u0, u1, u2, h, k)):
            coef_ref[slot, i] = value
        return ahead, now

    lax.fori_loop(0, rows, forward, ((zero,) * fields, (zero,) * fields), unroll=4)


def join_kernel(
    rows, partial_ref, coef_ref, even_x_ref, even_z_ref, odd_z_ref, odd_x_ref, arrive_ref, scale_ref,
    out_hbm, result, sems,
):
    x_even = lax.axis_index("gx") % 2 == 0
    z_even = lax.axis_index("gz") % 2 == 0
    per_segment = rows // segments
    wide = per_segment * 8
    left_sum = [jnp.where(x_even, odd_x_ref[c, 0], even_x_ref[c, 0]) for c in range(fields)]
    right_sum = [jnp.where(x_even, even_x_ref[c, 0], odd_x_ref[c, 0]) for c in range(fields)]

    def copy_out(s):
        part = pl.ds(s * per_segment, per_segment)
        return pltpu.make_async_copy(result.at[:, part], out_hbm.at[:, part], sems.at[s])

    def segment(s, carry):
        arrive = arrive_ref[...]
        lanes = pl.ds(pl.multiple_of(s * wide, wide), wide)
        span = []
        for c in range(fields):
            even = even_z_ref[c, :, lanes]
            odd = odd_z_ref[c, :, lanes]
            values = jnp.concatenate(
                [jnp.where(z_even, odd, even), jnp.where(z_even, even, odd)], 0
            )
            high = values.astype(jnp.bfloat16).astype(jnp.float32)
            low = values - high
            stacked = jnp.concatenate([high, low, high, jnp.zeros_like(high)], 0)
            columns = jnp.swapaxes(stacked, 0, 1).astype(jnp.bfloat16)
            span.append(
                jnp.dot(columns, arrive, preferred_element_type=jnp.float32).reshape(per_segment, 8, 128)
            )
        for j in range(per_segment):
            i = s * per_segment + j
            a = [left_sum[c] * scale_ref[0, i] + right_sum[c] * scale_ref[1, i] for c in range(fields)]
            if j == 0:
                edge = jnp.where(s == 0, -step_scale * side, 0.0).astype(jnp.float32)
                for c in range(fields):
                    a[c] = a[c] + edge * jnp.where(x_even, odd_x_ref[c, 1], even_x_ref[c, 1])
            if j == per_segment - 1:
                edge = jnp.where(s == segments - 1, step_scale * side, 0.0).astype(jnp.float32)
                for c in range(fields):
                    a[c] = a[c] + edge * jnp.where(x_even, even_x_ref[c, 1], odd_x_ref[c, 1])
            b = [span[c][j] for c in range(fields)]
            pulled = pull(a, b, *[coef_ref[slot, i] for slot in range(5)])
            for c in range(fields):
                result[c, i] = partial_ref[c, i] + pulled[c]
        copy_out(s).start()
        return carry

    lax.fori_loop(0, segments, segment, 0)

    def finish(s, carry):
        copy_out(s).wait()
        return carry

    lax.fori_loop(0, segments, finish, 0)


def per_device(density, momentum, energy, costate):
    rows, planes, cells = density.shape
    f32 = jnp.float32
    whole = pl.BlockSpec(memory_space=pltpu.VMEM)
    hbm = pl.BlockSpec(memory_space=pltpu.HBM)
    params = pltpu.CompilerParams(vmem_limit_bytes=vmem_bytes)
    x_shape = jax.ShapeDtypeStruct((fields, 2, planes, cells), f32)
    z_shape = jax.ShapeDtypeStruct((fields, 2, rows * planes), f32)
    block = jax.ShapeDtypeStruct((fields, rows, planes, cells), f32)
    per_segment = rows // segments

    held, even_x, even_z, odd_z, odd_x = pl.pallas_call(
        lambda *refs: ends_kernel(rows, *refs),
        out_shape=(
            jax.ShapeDtypeStruct((fields, segments, per_segment, planes, cells), f32),
            x_shape,
            z_shape,
            z_shape,
            x_shape,
        ),
        in_specs=[hbm, hbm],
        out_specs=(whole,) * 5,
        scratch_shapes=[
            pltpu.VMEM((16, cells), jnp.bfloat16),
            pltpu.SemaphoreType.DMA((fields + 1,)),
        ],
        compiler_params=params,
        name="ends",
    )(
        in_hbm(costate.reshape(fields, segments, per_segment, planes, cells)),
        in_hbm(jnp.asarray(stack_ends(end_weights(cells)))),
    )

    def pairs(values, axis, odd):
        count = lax.axis_size(axis)
        links = []
        for i in range(odd, count + odd, 2):
            a, b = i % count, (i + 1) % count
            links += [(a, b), (b, a)]
        return lax.ppermute(values, axis, links)

    even_x = pairs(even_x, "gx", 0)
    even_z = pairs(even_z, "gz", 0)
    odd_z = pairs(odd_z, "gz", 1)
    odd_x = pairs(odd_x, "gx", 1)

    matrix = local_matrix(cells)
    partial, coef = pl.pallas_call(
        lambda *refs: local_kernel(rows, *refs),
        out_shape=(block, block),
        in_specs=[whole] + [hbm] * 4,
        out_specs=(whole,) * 2,
        scratch_shapes=[
            pltpu.VMEM((fields, rows, planes, cells), f32),
            pltpu.VMEM((fields, rows, planes, cells), f32),
            pltpu.VMEM(matrix.shape, jnp.bfloat16),
            pltpu.VMEM((rows, planes, cells), f32),
            pltpu.VMEM((3, rows, planes, cells), f32),
            pltpu.VMEM((rows, planes, cells), f32),
            pltpu.SemaphoreType.DMA((4,)),
        ],
        compiler_params=params,
        cost_estimate=pl.CostEstimate(flops=300_000_000, bytes_accessed=10_000_000, transcendentals=0),
        name="local",
    )(
        held.reshape(costate.shape),
        in_hbm(jnp.asarray(matrix)),
        in_hbm(density),
        in_hbm(momentum),
        in_hbm(energy),
    )

    scale = jnp.asarray((step_scale * arrival_rows(rows)[0::2]).astype(np.float32))
    return pl.pallas_call(
        lambda *refs: join_kernel(rows, *refs),
        out_shape=block,
        in_specs=[whole] * 7 + [pl.BlockSpec(memory_space=pltpu.SMEM)],
        out_specs=hbm,
        scratch_shapes=[
            pltpu.VMEM((fields, rows, planes, cells), f32),
            pltpu.SemaphoreType.DMA((segments,)),
        ],
        compiler_params=params,
        name="join",
    )(
        partial,
        coef,
        even_x,
        even_z,
        odd_z,
        odd_x,
        jnp.asarray(stack_arrival(step_scale * arrival_rows(cells))),
        scale,
    )


def solution(mesh):
    return jax.shard_map(
        per_device,
        mesh=mesh,
        in_specs=(
            P("gx", None, "gz"),
            P(None, "gx", None, "gz"),
            P("gx", None, "gz"),
            P(None, "gx", None, "gz"),
        ),
        out_specs=P(None, "gx", None, "gz"),
        check_vma=False,
    )
```

time: 30.5 us -> 22.1 us (0.72)
  local copies, waits for them, and re-layouts: 5.08 us -> 0.01 us
  Pallas kernels: 12.9 us -> 10.9 us
  starting transfers between devices: 12.2 us -> 11 us
    unnamed x18 -> x4, local copies, waits for them, and re-layouts: 5.08 us -> 0.01 us
    pallas_call x1, Pallas kernels: 6.81 us -> 4.55 us  [per_device(): pl.pallas_call(lambda *refs: local_kernel(rows, *refs), out_shape=(block,...]
    ppermute x4, starting transfers between devices: 12.2 us -> 11 us  [pairs(): return lax.ppermute(values, axis, links)]
    pallas_call x1, Pallas kernels: 1.92 us -> 2.42 us  [per_device(): pl.pallas_call(lambda *refs: ends_kernel(rows, *refs), out_shape=(jax.Sha...]
  transfers between devices with their start and end apart: 4 -> 4, of which waited for: 0 -> 0; matrix products, arithmetic and copies ran while one was open for 0% -> 0% of each run, Pallas kernels for 23% -> 21%
where the time goes in v2:
time: 22.1 us; the launch traced here: 22 us
  starting transfers between devices  11 us (50%)
  Pallas kernels  10.9 us (49%)
    ppermute x4, starting transfers between devices, pairs(): return lax.ppermute(values, axis, links)  11 us
    pallas_call x1, Pallas kernels, per_device(): pl.pallas_call(lambda *refs: local_kernel(rows, *refs), out_shape=(block,...  4.55 us
    pallas_call x1, Pallas kernels, per_device(): pl.pallas_call(lambda *refs: join_kernel(rows, *refs), out_shape=block, i...  3.94 us
    pallas_call x1, Pallas kernels, per_device(): pl.pallas_call(lambda *refs: ends_kernel(rows, *refs), out_shape=(jax.Sha...  2.42 us
  transfers between devices with their start and end apart: 4, of which 0 were waited for; matrix products, arithmetic and copies ran while one was open for 0% of the time, Pallas kernels for 21%

profile of v2, /device:TPU:8, one launch (start us, length us, event | category | flops | bytes accessed | tf_op | source)
XLA Modules:
  0.0 22.0 jit_solution(4840745065895571448)
XLA Ops:
  0.0 2.4 %ends.1 = (f32[5,8,16,8,128]{4,3,2,1,0:T(8,128)S(1)}, f32[5,2,8,128]{3,2,1,0:T(8,128)S(1)}, f32[5,2,1024]{2,1,0:T(2,128)S(1)}, f32[5,2,1024]{2,1,0:T(2,128)S(1)}, f32[5,2,8,128]{3,2,1,0:T(8,128)S(1)}) custom-call(f32[5,8,16,8,128]{4,3,2,1,0:T(8,128)} %bitcast.3, bf16[16,128]{1,0:T(8,128)(2,1)} %constant.8.clone.refs_1_), custom_call_target="tpu_custom_call" | custom-call | tf_op jit(solution)/shard_map/ends/pallas_call | solution.py:292
  2.4 0.1 collective-permute-start
  2.5 1.6 %collective-permute-start.1 = (f32[5,2,1024]{2,1,0:T(2,128)S(1)}, f32[5,2,1024]{2,1,0:T(2,128)S(1)}, u32[]{:S(2)}, u32[]{:S(2)}) collective-permute-start(f32[5,2,1024]{2,1,0:T(2,128)S(1)} %get-tuple-element.16), channel_id=1, source_target_pairs={{0,1},{1,0},{2,3},{3,2},{4,5},{5,4},{6,7},{7,6},{8,9},{9,8},{10,11... | collective-permute-start | bytes 122888 | tf_op jit(solution)/shard_map/ppermute | solution.py:320
  4.1 2.0 %collective-permute-start.2 = (f32[5,2,1024]{2,1,0:T(2,128)S(1)}, f32[5,2,1024]{2,1,0:T(2,128)S(1)}, u32[]{:S(2)}, u32[]{:S(2)}) collective-permute-start(f32[5,2,1024]{2,1,0:T(2,128)S(1)} %get-tuple-element.17), channel_id=1, source_target_pairs={{1,2},{2,1},{3,4},{4,3},{5,6},{6,5},{7,0},{0,7},{9,10},{10,9},{11,... | collective-permute-start | bytes 122888 | tf_op jit(solution)/shard_map/ppermute | solution.py:320
  6.1 7.4 %collective-permute-start.3 = (f32[5,2,8,128]{3,2,1,0:T(8,128)S(1)}, f32[5,2,8,128]{3,2,1,0:T(8,128)S(1)}, u32[]{:S(2)}, u32[]{:S(2)}) collective-permute-start(f32[5,2,8,128]{3,2,1,0:T(8,128)S(1)} %get-tuple-element.18), channel_id=1, source_target_pairs={{8,16},{16,8},{24,32},{32,24},{40,48},{48,40},{56,64},{64,56},{72,... | collective-permute-start | bytes 122888 | tf_op jit(solution)/shard_map/ppermute | solution.py:320
  13.4 0.0 copy-start
  13.4 0.0 copy-start.1
  13.5 4.5 %local.1 = (f32[5,128,8,128]{3,2,1,0:T(8,128)S(1)}, f32[5,128,8,128]{3,2,1,0:T(8,128)S(1)}) custom-call(f32[5,128,8,128]{3,2,1,0:T(8,128)S(1)} %bitcast.2, bf16[256,256]{1,0:T(8,128)(2,1)} %constant.9.clone.refs_1_, f32[128,8,128]{2,1,0:T(8,128)} %refs_2_.1, f32[3,128,8,128]{3,2,1,0:T(8,128)} %refs_3_.1, f32[128,8,128]{2,1,0:T(8,128)} %refs_4_.1), custom_call_target="tpu_custom_call" | custom-call | flops 300000000 | bytes 10000000 | tf_op jit(solution)/shard_map/local/pallas_call | solution.py:328
  18.0 0.0 collective-permute-done.refs_2_
  18.0 0.0 collective-permute-done.1.refs_3_
  18.0 0.0 collective-permute-done.2.refs_4_
  18.0 0.0 collective-permute-done.3.refs_5_
  18.1 0.0 copy-done
  18.1 0.0 copy-done.1
  18.1 3.9 %join.1 = f32[5,128,8,128]{3,2,1,0:T(8,128)} custom-call(f32[5,128,8,128]{3,2,1,0:T(8,128)S(1)} %get-tuple-element.13.refs_0_, f32[5,128,8,128]{3,2,1,0:T(8,128)S(1)} %get-tuple-element.14.refs_1_, f32[5,2,8,128]{3,2,1,0:T(8,128)S(1)} %collective-permute-done.refs_2_, f32[5,2,1024]{2,1,0:T(2,128)S(1)} %collective-permute-done.1.refs_3_, ...), custom_call_target="tpu_custom_call" | custom-call | tf_op jit(solution)/shard_map/join/pallas_call | solution.py:354
Async XLA Ops:
  2.4 15.6 %collective-permute-start = (f32[5,2,8,128]{3,2,1,0:T(8,128)S(1)}, f32[5,2,8,128]{3,2,1,0:T(8,128)S(1)}, u32[]{:S(2)}, u32[]{:S(2)}) collective-permute-start(f32[5,2,8,128]{3,2,1,0:T(8,128)S(1)} %get-tuple-element.15), channel_id=1, source_target_pairs={{0,8},{8,0},{16,24},{24,16},{32,40},{40,32},{48,56},{56,48},{64,72... | collective-permute-start | bytes 122888 | tf_op jit(solution)/shard_map/ppermute | solution.py:320
  2.5 15.5 %collective-permute-start.1 = (f32[5,2,1024]{2,1,0:T(2,128)S(1)}, f32[5,2,1024]{2,1,0:T(2,128)S(1)}, u32[]{:S(2)}, u32[]{:S(2)}) collective-permute-start(f32[5,2,1024]{2,1,0:T(2,128)S(1)} %get-tuple-element.16), channel_id=1, source_target_pairs={{0,1},{1,0},{2,3},{3,2},{4,5},{5,4},{6,7},{7,6},{8,9},{9,8},{10,11... | collective-permute-start | bytes 122888 | tf_op jit(solution)/shard_map/ppermute | solution.py:320
  4.1 13.9 %collective-permute-start.2 = (f32[5,2,1024]{2,1,0:T(2,128)S(1)}, f32[5,2,1024]{2,1,0:T(2,128)S(1)}, u32[]{:S(2)}, u32[]{:S(2)}) collective-permute-start(f32[5,2,1024]{2,1,0:T(2,128)S(1)} %get-tuple-element.17), channel_id=1, source_target_pairs={{1,2},{2,1},{3,4},{4,3},{5,6},{6,5},{7,0},{0,7},{9,10},{10,9},{11,... | collective-permute-start | bytes 122888 | tf_op jit(solution)/shard_map/ppermute | solution.py:320
  6.1 12.0 %collective-permute-start.3 = (f32[5,2,8,128]{3,2,1,0:T(8,128)S(1)}, f32[5,2,8,128]{3,2,1,0:T(8,128)S(1)}, u32[]{:S(2)}, u32[]{:S(2)}) collective-permute-start(f32[5,2,8,128]{3,2,1,0:T(8,128)S(1)} %get-tuple-element.18), channel_id=1, source_target_pairs={{8,16},{16,8},{24,32},{32,24},{40,48},{48,40},{56,64},{64,56},{72,... | collective-permute-start | bytes 122888 | tf_op jit(solution)/shard_map/ppermute | solution.py:320
  13.4 4.6 %copy-start = (bf16[16,128]{1,0:T(8,128)(2,1)S(1)}, bf16[16,128]{1,0:T(8,128)(2,1)}, u32[]{:S(2)}) copy-start(bf16[16,128]{1,0:T(8,128)(2,1)} %constant.11.clone.refs_6_) | copy-start | bytes 12292
  13.4 4.6 %copy-start.1 = (f32[2,128]{1,0:T(2,128)S(1)}, f32[2,128]{1,0:T(2,128)}, u32[]{:S(2)}) copy-start(f32[2,128]{1,0:T(2,128)} %constant.10.clone.refs_7_) | copy-start | bytes 3076

commit v3 on v2

v3 whole, which is shorter than its diff:
```python
import math

import jax
import jax.numpy as jnp
import ml_dtypes
import numpy as np
from jax import lax
from jax.experimental import pallas as pl
from jax.experimental.pallas import tpu as pltpu
from jax.sharding import PartitionSpec as P

pade_alpha = 1.0 / 3.0
near_coef = 14.0 / 9.0
far_coef = 1.0 / 9.0
step_scale = 0.1
gas_gamma = 1.4

root = (-1.0 + math.sqrt(1.0 - 4.0 * pade_alpha * pade_alpha)) / (2.0 * pade_alpha)
side = 0.25 * far_coef / pade_alpha
tail = (0.5 * near_coef - side) / pade_alpha

fields = 5
segments = 8
arrival_depth = 24
vmem_bytes = 16 * 1024 * 1024


def split(values):
    high = values.astype(ml_dtypes.bfloat16)
    low = (values - high.astype(np.float64)).astype(ml_dtypes.bfloat16)
    return high, low


def end_weights(length):
    cell = np.arange(length, dtype=np.float64)
    rows = np.zeros((4, length))
    rows[0] = root ** (length - cell)
    rows[1, length - 1] = 1.0
    rows[2] = root ** (cell + 1.0)
    rows[3, 0] = 1.0
    return rows


def stack_ends(rows):
    stacked = np.zeros((2, 16, 2 * rows.shape[1]), ml_dtypes.bfloat16)
    for place, order in enumerate(((0, 1, 2, 3), (2, 3, 0, 1))):
        high, low = split(rows[list(order)])
        stacked[place, 0:4] = np.concatenate([high, high], 1)
        stacked[place, 8:12] = np.concatenate([low, np.zeros_like(low)], 1)
    return stacked


def local_matrix(length):
    cell = np.arange(length)
    gap = cell[None, :] - cell[:, None]
    reach = np.abs(gap).astype(np.float64)
    taps = np.where(reach > 0, tail * root**reach, 0.0) - np.where(reach == 1, side, 0.0)
    high, low = split(step_scale * np.sign(gap) * taps)
    return np.concatenate(
        [np.concatenate([high, low], 1), np.concatenate([high, low], 1)], 0
    )


def arrival_rows(length):
    cell = np.arange(length, dtype=np.float64)
    rows = np.zeros((4, length))
    rows[0] = tail * root**cell
    rows[1, 0] = -side
    rows[2] = -tail * root ** (length - 1.0 - cell)
    rows[3, length - 1] = side
    return rows


def stack_arrival(rows):
    length = rows.shape[1]
    stacked = np.zeros((2, 3 * arrival_depth, fields * length), ml_dtypes.bfloat16)
    for place, order in enumerate(((2, 3, 0, 1), (0, 1, 2, 3))):
        high, low = split(rows[list(order)])
        for n in range(4):
            for c in range(fields):
                at = (n // 2) * 2 * fields + 2 * c + n % 2
                lanes = slice(c * length, (c + 1) * length)
                stacked[place, at, lanes] = high[n]
                stacked[place, arrival_depth + at, lanes] = high[n]
                stacked[place, 2 * arrival_depth + at, lanes] = low[n]
    return stacked


def in_hbm(values):
    return pltpu.with_memory_space_constraint(values, pltpu.HBM)


def ends_kernel(
    rows, costate_hbm, weights_hbm, matrix_hbm, arrive_hbm, held, even_x_ref, even_z_ref, odd_z_ref,
    odd_x_ref, matrix_ref, arrive_ref, weights_ref, sems,
):
    per_segment = rows // segments
    place = lax.axis_index("gz") % 2
    constants = [
        pltpu.make_async_copy(source, target, sems.at[fields + n])
        for n, (source, target) in enumerate(
            (
                (weights_hbm.at[place], weights_ref),
                (matrix_hbm, matrix_ref),
                (arrive_hbm.at[place], arrive_ref),
            )
        )
    ]
    constants[0].start()
    for c in range(fields):
        pltpu.make_async_copy(costate_hbm.at[c], held.at[c], sems.at[c]).start()
    constants[1].start()
    constants[2].start()
    x_even = lax.axis_index("gx") % 2 == 0
    constants[0].wait()

    def component(c, carry):
        pltpu.make_async_copy(costate_hbm.at[c], held.at[c], sems.at[c]).wait()
        lines = held[c].reshape(-1, 128)
        high = lines.astype(jnp.bfloat16)
        low = (lines - high.astype(jnp.float32)).astype(jnp.bfloat16)
        sums = lax.dot_general(
            weights_ref[...],
            jnp.concatenate([high, low], 1),
            (((1,), (1,)), ((), ())),
            preferred_element_type=jnp.float32,
        )
        sums = sums[0:8] + sums[8:16]
        even_z_ref[c] = sums[0:2]
        odd_z_ref[c] = sums[2:4]
        ahead = held[c, :, 0]
        back = held[c, :, per_segment - 1]
        for j in range(1, per_segment):
            ahead = ahead * root + held[c, :, j]
            back = back * root + held[c, :, per_segment - 1 - j]
        right = [ahead[segments - 1 - s] * float(root ** (1 + s * per_segment)) for s in range(segments)]
        left = [back[s] * float(root ** (1 + s * per_segment)) for s in range(segments)]
        while len(right) > 1:
            right = [right[n] + right[n + 1] for n in range(0, len(right), 2)]
            left = [left[n] + left[n + 1] for n in range(0, len(left), 2)]
        first = held[c, 0, 0]
        last = held[c, segments - 1, per_segment - 1]
        even_x_ref[c, 0] = jnp.where(x_even, right[0], left[0])
        even_x_ref[c, 1] = jnp.where(x_even, last, first)
        odd_x_ref[c, 0] = jnp.where(x_even, left[0], right[0])
        odd_x_ref[c, 1] = jnp.where(x_even, first, last)
        return carry

    lax.fori_loop(0, fields, component, 0)
    constants[1].wait()
    constants[2].wait()


def pull(a, b, u0, u1, u2, h, k):
    a4u0 = a[4] * u0
    b4u2 = b[4] * u2
    both = a4u0 + b4u2
    g = (gas_gamma - 1.0) * (a[1] + b[3] + both)
    a1u0 = a[1] * u0
    b3u2 = b[3] * u2
    v0 = a1u0 + a[2] * u1 + a[3] * u2 + a[4] * h
    v2 = b[1] * u0 + b[2] * u1 + b3u2 + b[4] * h
    mass = g * k - v0 * u0 - v2 * u2
    m0 = a[0] + a1u0 + b[1] * u2 + v0 - g * u0
    m1 = a[2] * u0 + b[2] * u2 - g * u1
    m2 = b[0] + a[3] * u0 + b3u2 + v2 - g * u2
    energy = both + g
    return [mass, m0, m1, m2, energy]


def slope_body(
    rows, costate_ref, even_x_ref, matrix_ref, density_hbm, momentum_hbm, energy_hbm,
    stream_ref, span_ref, coef_ref, density_ref, momentum_ref, energy_ref, sems,
):
    copies = [
        pltpu.make_async_copy(source, target, sems.at[n])
        for n, (source, target) in enumerate(
            (
                (density_hbm, density_ref),
                (momentum_hbm, momentum_ref),
                (energy_hbm, energy_ref),
            )
        )
    ]
    for copy in copies:
        copy.start()
    x_even = lax.axis_index("gx") % 2 == 0
    gain = step_scale * tail
    edge = step_scale * side
    from_right = jnp.where(x_even, 1.0, 0.0).astype(jnp.float32)
    from_left = 1.0 - from_right
    right_sum = tuple(even_x_ref[c, 0] * (from_right * gain) for c in range(fields))
    for c in range(fields):
        stream_ref[c, rows - 1] = right_sum[c] - even_x_ref[c, 1] * (from_right * edge)

    def backward(step, carry):
        i = rows - 2 - step
        nxt = []
        for c in range(fields):
            after = costate_ref[c, i + 1]
            now = carry[c] * root + after * (gain * root)
            stream_ref[c, i] = now - after * edge
            nxt.append(now)
        return tuple(nxt)

    lax.fori_loop(0, rows - 1, backward, right_sum, unroll=8)

    def across(c, carry):
        lines = costate_ref[c].reshape(-1, 128)
        high = lines.astype(jnp.bfloat16)
        low = (lines - high.astype(jnp.float32)).astype(jnp.bfloat16)
        out = jnp.dot(
            jnp.concatenate([high, low], 1), matrix_ref[...], preferred_element_type=jnp.float32
        )
        span_ref[c] = (out[:, :128] + out[:, 128:]).reshape(rows, 8, 128)
        return carry

    lax.fori_loop(0, fields, across, 0)
    for copy in copies:
        copy.wait()

    def forward(i, carry):
        ahead, before = carry
        rho = density_ref[i]
        inverse = pl.reciprocal(rho, approx=True)
        inverse = inverse * (2.0 - rho * inverse)
        inverse = inverse * (2.0 - rho * inverse)
        u0 = momentum_ref[0, i] * inverse
        u1 = momentum_ref[1, i] * inverse
        u2 = momentum_ref[2, i] * inverse
        k = 0.5 * (u0 * u0 + u1 * u1 + u2 * u2)
        h = gas_gamma * (energy_ref[i] * inverse) - (gas_gamma - 1.0) * k
        for slot, value in enumerate((u0, u1, u2, h, k)):
            coef_ref[slot, i] = value
        ahead = tuple(ahead[c] * root + before[c] * (gain * root) for c in range(fields))
        for c in range(fields):
            stream_ref[c, i] = ahead[c] - before[c] * edge - stream_ref[c, i]
        return ahead, tuple(costate_ref[c, i] for c in range(fields))

    before = tuple(even_x_ref[c, 1] * from_left for c in range(fields))
    ahead = tuple(
        (even_x_ref[c, 0] * (from_left / root) - before[c]) * gain for c in range(fields)
    )
    lax.fori_loop(0, rows, forward, (ahead, before), unroll=4)


def early_slope_kernel(rows, *refs):
    odd_x_in, refs = refs[6], refs[:6] + refs[7:]
    odd_x_out, refs = refs[9], refs[:9] + refs[10:]

    @pl.when(lax.axis_index("gx") == 0)
    def _():
        slope_body(rows, *refs)


def late_slope_kernel(rows, *refs):
    refs = refs[:6] + refs[9:]

    @pl.when(lax.axis_index("gx") != 0)
    def _():
        slope_body(rows, *refs)


def gather_kernel(
    rows, costate_ref, stream_ref, span_ref, coef_ref, even_z_ref, odd_z_ref, arrive_ref,
    partial_ref, values, arrived,
):
    count = 2 * fields
    half = rows // 2
    width = half * 8
    values[16:24] = jnp.zeros((8, values.shape[1]), jnp.float32)
    for c in range(fields):
        values[2 * c : 2 * c + 2] = even_z_ref[c]
        values[count + 2 * c : count + 2 * c + 2] = odd_z_ref[c]
    for part in range(2):
        whole = values[:, part * width : (part + 1) * width]
        top = whole.astype(jnp.bfloat16).astype(jnp.float32)
        stacked = jnp.concatenate([top, whole - top, top], 0)
        columns = jnp.swapaxes(stacked, 0, 1).astype(jnp.bfloat16)
        out = jnp.dot(columns, arrive_ref[...], preferred_element_type=jnp.float32)
        for c in range(fields):
            arrived[c, part * half : (part + 1) * half] = out[:, c * 128 : (c + 1) * 128].reshape(
                half, 8, 128
            )

    def add(i, carry):
        a = [stream_ref[c, i] for c in range(fields)]
        b = [span_ref[c, i] + arrived[c, i] for c in range(fields)]
        pulled = pull(a, b, *[coef_ref[slot, i] for slot in range(5)])
        for c in range(fields):
            partial_ref[c, i] = costate_ref[c, i] + pulled[c]
        return carry

    lax.fori_loop(0, rows, add, 0, unroll=4)


def pull_stream(a, u0, u1, u2, h, k):
    both = a[4] * u0
    g = (gas_gamma - 1.0) * (a[1] + both)
    a1u0 = a[1] * u0
    v0 = a1u0 + a[2] * u1 + a[3] * u2 + a[4] * h
    return [
        g * k - v0 * u0,
        a[0] + a1u0 + v0 - g * u0,
        a[2] * u0 - g * u1,
        a[3] * u0 - g * u2,
        both + g,
    ]


def join_kernel(rows, partial_ref, coef_ref, odd_x_ref, out_hbm, result, sems):
    place = lax.axis_index("gx") % 2
    per_segment = rows // segments
    sign = jnp.where(place == 0, 1.0, -1.0).astype(jnp.float32)

    def copy_out(s):
        at = jnp.where(place == 0, s, segments - 1 - s)
        part = pl.ds(at * per_segment, per_segment)
        return pltpu.make_async_copy(result.at[:, part], out_hbm.at[:, part], sems.at[s])

    def step(t, a):
        i = jnp.where(place == 0, t, rows - 1 - t)
        pulled = pull_stream(a, *[coef_ref[slot, i] for slot in range(5)])
        for c in range(fields):
            result[c, i] = partial_ref[c, i] + pulled[c]

    def segment(s, carry):
        for j in range(per_segment):
            now = carry
            if j == 0:
                edge = jnp.where(s == 0, -sign * (step_scale * side), 0.0).astype(jnp.float32)
                now = tuple(carry[c] + edge * odd_x_ref[c, 1] for c in range(fields))
            step(s * per_segment + j, now)
            carry = tuple(value * root for value in carry)
        copy_out(s).start()
        return carry

    total = tuple(odd_x_ref[c, 0] * (sign * (step_scale * tail)) for c in range(fields))
    lax.fori_loop(0, segments, segment, total)

    def finish(s, carry):
        copy_out(s).wait()
        return carry

    lax.fori_loop(0, segments, finish, 0)


def per_device(density, momentum, energy, costate):
    rows, planes, cells = density.shape
    f32 = jnp.float32
    whole = pl.BlockSpec(memory_space=pltpu.VMEM)
    hbm = pl.BlockSpec(memory_space=pltpu.HBM)
    params = pltpu.CompilerParams(vmem_limit_bytes=vmem_bytes)
    x_shape = jax.ShapeDtypeStruct((fields, 2, planes, cells), f32)
    z_shape = jax.ShapeDtypeStruct((fields, 2, rows * planes), f32)
    block = jax.ShapeDtypeStruct((fields, rows, planes, cells), f32)
    per_segment = rows // segments

    matrix = local_matrix(cells)
    arrive = stack_arrival(step_scale * arrival_rows(cells))
    held, even_x, even_z, odd_z, odd_x, matrix, arrive = pl.pallas_call(
        lambda *refs: ends_kernel(rows, *refs),
        out_shape=(
            jax.ShapeDtypeStruct((fields, segments, per_segment, planes, cells), f32),
            x_shape,
            z_shape,
            z_shape,
            x_shape,
            jax.ShapeDtypeStruct(matrix.shape, jnp.bfloat16),
            jax.ShapeDtypeStruct(arrive.shape[1:], jnp.bfloat16),
        ),
        in_specs=[hbm] * 4,
        out_specs=(whole,) * 7,
        scratch_shapes=[
            pltpu.VMEM((16, 2 * cells), jnp.bfloat16),
            pltpu.SemaphoreType.DMA((fields + 3,)),
        ],
        compiler_params=params,
        name="ends",
    )(
        in_hbm(costate.reshape(fields, segments, per_segment, planes, cells)),
        in_hbm(jnp.asarray(stack_ends(end_weights(cells)))),
        in_hbm(jnp.asarray(matrix)),
        in_hbm(jnp.asarray(arrive)),
    )
    held = held.reshape(costate.shape)

    def pairs(values, axis, odd):
        count = lax.axis_size(axis)
        links = []
        for i in range(odd, count + odd, 2):
            a, b = i % count, (i + 1) % count
            links += [(a, b), (b, a)]
        return lax.ppermute(values, axis, links)

    even_x = pairs(even_x, "gx", 0)
    even_z = pairs(even_z, "gz", 0)
    odd_z = pairs(odd_z, "gz", 1)

    state = (
        pltpu.VMEM((rows, planes, cells), f32),
        pltpu.VMEM((3, rows, planes, cells), f32),
        pltpu.VMEM((rows, planes, cells), f32),
    )
    inputs = (held, even_x, matrix, in_hbm(density), in_hbm(momentum), in_hbm(energy))
    stream, span, coef, odd_x = pl.pallas_call(
        lambda *refs: early_slope_kernel(rows, *refs),
        out_shape=(block, block, block, x_shape),
        in_specs=[whole] * 3 + [hbm] * 3 + [whole],
        out_specs=(whole,) * 4,
        scratch_shapes=[*state, pltpu.SemaphoreType.DMA((3,))],
        input_output_aliases={6: 3},
        compiler_params=params,
        name="early_slope",
    )(*inputs, odd_x)

    odd_x = pairs(odd_x, "gx", 1)

    stream, span, coef = pl.pallas_call(
        lambda *refs: late_slope_kernel(rows, *refs),
        out_shape=(block,) * 3,
        in_specs=[whole] * 3 + [hbm] * 3 + [whole] * 3,
        out_specs=(whole,) * 3,
        scratch_shapes=[*state, pltpu.SemaphoreType.DMA((3,))],
        input_output_aliases={6: 0, 7: 1, 8: 2},
        compiler_params=params,
        cost_estimate=pl.CostEstimate(flops=300_000_000, bytes_accessed=10_000_000, transcendentals=0),
        name="late_slope",
    )(*inputs, stream, span, coef)

    partial = pl.pallas_call(
        lambda *refs: gather_kernel(rows, *refs),
        out_shape=block,
        in_specs=[whole] * 7,
        out_specs=whole,
        scratch_shapes=[
            pltpu.VMEM((arrival_depth, rows * planes), f32),
            pltpu.VMEM((fields, rows, planes, cells), f32),
        ],
        compiler_params=params,
        cost_estimate=pl.CostEstimate(flops=100_000_000, bytes_accessed=10_000_000, transcendentals=0),
        name="gather",
    )(held, stream, span, coef, even_z, odd_z, arrive)

    return pl.pallas_call(
        lambda *refs: join_kernel(rows, *refs),
        out_shape=block,
        in_specs=[whole] * 3,
        out_specs=hbm,
        scratch_shapes=[
            pltpu.VMEM((fields, rows, planes, cells), f32),
            pltpu.SemaphoreType.DMA((segments,)),
        ],
        compiler_params=params,
        name="join",
    )(partial, coef, odd_x)


def solution(mesh):
    return jax.shard_map(
        per_device,
        mesh=mesh,
        in_specs=(
            P("gx", None, "gz"),
            P(None, "gx", None, "gz"),
            P("gx", None, "gz"),
            P(None, "gx", None, "gz"),
        ),
        out_specs=P(None, "gx", None, "gz"),
        check_vma=False,
    )
```

time: 22.1 us -> 18.7 us (0.85)
  starting transfers between devices: 11 us -> 7.66 us
  Pallas kernels: 10.9 us -> 9.61 us
  waiting for transfers between devices: 0.01 us -> 1.24 us
    ppermute x4, starting transfers between devices: 11 us -> 7.66 us  [pairs(): return lax.ppermute(values, axis, links)]
    pallas_call x1, Pallas kernels: 3.94 us -> 1.86 us  [per_device(): pl.pallas_call(lambda *refs: join_kernel(rows, *refs), out_shape=block, i...]
    ppermute x4, waiting for transfers between devices: 0.01 us -> 1.24 us  [pairs(): return lax.ppermute(values, axis, links)]
    pallas_call x1 -> x3, Pallas kernels: 4.55 us -> 5.31 us  [the longest x1 3.46 us: per_device(): pl.pallas_call(lambda *refs: early_slope_kernel(rows, *refs), out_shape=(...]
  transfers between devices with their start and end apart: 4 -> 4, of which waited for: 0 -> 1; matrix products, arithmetic and copies ran while one was open for 0% -> 0% of each run, Pallas kernels for 21% -> 29%
where the time goes in v3:
time: 18.7 us; the launch traced here: 18.6 us
  Pallas kernels  9.61 us (51%)
  starting transfers between devices  7.66 us (41%)
  waiting for transfers between devices  1.24 us (7%)
    ppermute x4, starting transfers between devices, pairs(): return lax.ppermute(values, axis, links)  7.66 us
    pallas_call x1, Pallas kernels, per_device(): pl.pallas_call(lambda *refs: early_slope_kernel(rows, *refs), out_shape=(...  3.46 us
    pallas_call x1, Pallas kernels, per_device(): pl.pallas_call(lambda *refs: ends_kernel(rows, *refs), out_shape=(jax.Sha...  2.44 us
    pallas_call x1, Pallas kernels, per_device(): pl.pallas_call(lambda *refs: join_kernel(rows, *refs), out_shape=block, i...  1.86 us
    pallas_call x1, Pallas kernels, per_device(): pl.pallas_call(lambda *refs: gather_kernel(rows, *refs), out_shape=block,...  1.83 us
    ppermute x4, waiting for transfers between devices, pairs(): return lax.ppermute(values, axis, links)  1.24 us
  transfers between devices with their start and end apart: 4, of which 1 were waited for; matrix products, arithmetic and copies ran while one was open for 0% of the time, Pallas kernels for 29%

profile of v3, /device:TPU:8, one launch (start us, length us, event | category | flops | bytes accessed | tf_op | source)
XLA Modules:
  0.0 18.6 jit_solution(2174557294871480839)
XLA Ops:
  0.0 2.4 %ends.1 = (f32[5,8,16,8,128]{4,3,2,1,0:T(8,128)S(1)}, f32[5,2,8,128]{3,2,1,0:T(8,128)S(1)}, f32[5,2,1024]{2,1,0:T(2,128)S(1)}, f32[5,2,1024]{2,1,0:T(2,128)S(1)}...) custom-call(f32[5,8,16,8,128]{4,3,2,1,0:T(8,128)} %bitcast.5, ...), custom_call_target="tpu_custom_call" | custom-call | tf_op jit(solution)/shard_map/ends/pallas_call | solution.py:361
  2.4 0.1 collective-permute-start
  2.5 1.6 %collective-permute-start.1 = (f32[5,2,1024]{2,1,0:T(2,128)S(1)}, f32[5,2,1024]{2,1,0:T(2,128)S(1)}, u32[]{:S(2)}, u32[]{:S(2)}) collective-permute-start(f32[5,2,1024]{2,1,0:T(2,128)S(1)} %get-tuple-element.29), channel_id=1, source_target_pairs={{0,1},{1,0},{2,3},{3,2},{4,5},{5,4},{6,7},{7,6},{8,9},{9,8},{10,11... | collective-permute-start | bytes 122888 | tf_op jit(solution)/shard_map/ppermute | solution.py:394
  4.1 2.0 %collective-permute-start.2 = (f32[5,2,1024]{2,1,0:T(2,128)S(1)}, f32[5,2,1024]{2,1,0:T(2,128)S(1)}, u32[]{:S(2)}, u32[]{:S(2)}) collective-permute-start(f32[5,2,1024]{2,1,0:T(2,128)S(1)} %get-tuple-element.30), channel_id=1, source_target_pairs={{1,2},{2,1},{3,4},{4,3},{5,6},{6,5},{7,0},{0,7},{9,10},{10,9},{11,... | collective-permute-start | bytes 122888 | tf_op jit(solution)/shard_map/ppermute | solution.py:394
  6.1 0.0 collective-permute-done.refs_1_
  6.1 3.5 %early_slope.1 = (f32[5,128,8,128]{3,2,1,0:T(8,128)S(1)}, f32[5,128,8,128]{3,2,1,0:T(8,128)S(1)}, f32[5,128,8,128]{3,2,1,0:T(8,128)S(1)}, f32[5,2,8,128]{3,2,1,0:T(8,128)S(1)}) custom-call(f32[5,128,8,128]{3,2,1,0:T(8,128)S(1)} %bitcast.2, f32[5,2,8,128]{3,2,1,0:T(8,128)S(1)} %collective-permute-done.refs_1_, ...), custom_call_target="tpu_custom_call", output_to_operand_aliasing={{3}: (6, {})} | custom-call | tf_op jit(solution)/shard_map/early_slope/pallas_call | solution.py:406
  9.6 4.0 %collective-permute-start.3 = (f32[5,2,8,128]{3,2,1,0:T(8,128)S(1)}, f32[5,2,8,128]{3,2,1,0:T(8,128)S(1)}, u32[]{:S(2)}, u32[]{:S(2)}) collective-permute-start(f32[5,2,8,128]{3,2,1,0:T(8,128)S(1)} %get-tuple-element.32), channel_id=1, source_target_pairs={{8,16},{16,8},{24,32},{32,24},{40,48},{48,40},{56,64},{64,56},{72,... | collective-permute-start | bytes 122888 | tf_op jit(solution)/shard_map/ppermute | solution.py:394
  13.6 0.0 collective-permute-done.1.refs_4_
  13.6 0.0 collective-permute-done.2.refs_5_
  13.6 1.8 %gather.1.refs_0_ = f32[5,128,8,128]{3,2,1,0:T(8,128)S(1)} custom-call(f32[5,128,8,128]{3,2,1,0:T(8,128)S(1)} %bitcast.4, f32[5,128,8,128]{3,2,1,0:T(8,128)S(1)} %get-tuple-element.26.refs_1_, f32[5,128,8,128]{3,2,1,0:T(8,128)S(1)} %get-tuple-element.27.refs_2_, f32[5,128,8,128]{3,2,1,0:T(8,128)S(1)} %get-tuple-element.28.refs_3_.refs_1_, ...), custom_call_target="tpu_custom_call" | custom-call | flops 100000000 | bytes 10000000 | tf_op jit(solution)/shard_map/gather/pallas_call | solution.py:431
  15.5 1.2 %collective-permute-done.3.refs_2_ = f32[5,2,8,128]{3,2,1,0:T(8,128)S(1)} collective-permute-done((f32[5,2,8,128]{3,2,1,0:T(8,128)S(1)}, f32[5,2,8,128]{3,2,1,0:T(8,128)S(1)}, u32[]{:S(2)}, u32[]{:S(2)}) %collective-permute-start.3) | collective-permute-done | bytes 40992 | tf_op jit(solution)/shard_map/ppermute | solution.py:394
  16.7 1.9 %join.1 = f32[5,128,8,128]{3,2,1,0:T(8,128)} custom-call(f32[5,128,8,128]{3,2,1,0:T(8,128)S(1)} %gather.1.refs_0_, f32[5,128,8,128]{3,2,1,0:T(8,128)S(1)} %get-tuple-element.28.refs_3_.refs_1_, f32[5,2,8,128]{3,2,1,0:T(8,128)S(1)} %collective-permute-done.3.refs_2_), custom_call_target="tpu_custom_call" | custom-call | tf_op jit(solution)/shard_map/join/pallas_call | solution.py:445
  (1 shorter events, 0.0 us)
Async XLA Ops:
  2.4 3.7 %collective-permute-start = (f32[5,2,8,128]{3,2,1,0:T(8,128)S(1)}, f32[5,2,8,128]{3,2,1,0:T(8,128)S(1)}, u32[]{:S(2)}, u32[]{:S(2)}) collective-permute-start(f32[5,2,8,128]{3,2,1,0:T(8,128)S(1)} %get-tuple-element.20), channel_id=1, source_target_pairs={{0,8},{8,0},{16,24},{24,16},{32,40},{40,32},{48,56},{56,48},{64,72... | collective-permute-start | bytes 122888 | tf_op jit(solution)/shard_map/ppermute | solution.py:394
  2.5 11.1 %collective-permute-start.1 = (f32[5,2,1024]{2,1,0:T(2,128)S(1)}, f32[5,2,1024]{2,1,0:T(2,128)S(1)}, u32[]{:S(2)}, u32[]{:S(2)}) collective-permute-start(f32[5,2,1024]{2,1,0:T(2,128)S(1)} %get-tuple-element.29), channel_id=1, source_target_pairs={{0,1},{1,0},{2,3},{3,2},{4,5},{5,4},{6,7},{7,6},{8,9},{9,8},{10,11... | collective-permute-start | bytes 122888 | tf_op jit(solution)/shard_map/ppermute | solution.py:394
  4.1 9.5 %collective-permute-start.2 = (f32[5,2,1024]{2,1,0:T(2,128)S(1)}, f32[5,2,1024]{2,1,0:T(2,128)S(1)}, u32[]{:S(2)}, u32[]{:S(2)}) collective-permute-start(f32[5,2,1024]{2,1,0:T(2,128)S(1)} %get-tuple-element.30), channel_id=1, source_target_pairs={{1,2},{2,1},{3,4},{4,3},{5,6},{6,5},{7,0},{0,7},{9,10},{10,9},{11,... | collective-permute-start | bytes 122888 | tf_op jit(solution)/shard_map/ppermute | solution.py:394
  9.6 7.1 %collective-permute-start.3 = (f32[5,2,8,128]{3,2,1,0:T(8,128)S(1)}, f32[5,2,8,128]{3,2,1,0:T(8,128)S(1)}, u32[]{:S(2)}, u32[]{:S(2)}) collective-permute-start(f32[5,2,8,128]{3,2,1,0:T(8,128)S(1)} %get-tuple-element.32), channel_id=1, source_target_pairs={{8,16},{16,8},{24,32},{32,24},{40,48},{48,40},{56,64},{64,56},{72,... | collective-permute-start | bytes 122888 | tf_op jit(solution)/shard_map/ppermute | solution.py:394

commit v4 on v3

--- a/solution.py
+++ b/solution.py
@@ -206,24 +206,34 @@
     lax.fori_loop(0, rows - 1, backward, right_sum, unroll=8)
 
     def across(c, carry):
-        lines = costate_ref[c].reshape(-1, 128)
+        lines = costate_ref[...].reshape(-1, 128)
         high = lines.astype(jnp.bfloat16)
         low = (lines - high.astype(jnp.float32)).astype(jnp.bfloat16)
         out = jnp.dot(
             jnp.concatenate([high, low], 1), matrix_ref[...], preferred_element_type=jnp.float32
         )
-        span_ref[c] = (out[:, :128] + out[:, 128:]).reshape(rows, 8, 128)
-        return carry
-
-    lax.fori_loop(0, fields, across, 0)
+        span_ref[...] = (out[:, :128] + out[:, 128:]).reshape(fields, rows, 8, 128)
+        return carry
+
+    across(0, 0)
+    def forward(i, carry):
+        ahead, before = carry
+        ahead = tuple(ahead[c] * root + before[c] * (gain * root) for c in range(fields))
+        for c in range(fields):
+            stream_ref[c, i] = ahead[c] - before[c] * edge - stream_ref[c, i]
+        return ahead, tuple(costate_ref[c, i] for c in range(fields))
+
+    before = tuple(even_x_ref[c, 1] * from_left for c in range(fields))
+    ahead = tuple(
+        (even_x_ref[c, 0] * (from_left / root) - before[c]) * gain for c in range(fields)
+    )
+    lax.fori_loop(0, rows, forward, (ahead, before), unroll=8)
     for copy in copies:
         copy.wait()
 
-    def forward(i, carry):
-        ahead, before = carry
+    def state(i, carry):
         rho = density_ref[i]
         inverse = pl.reciprocal(rho, approx=True)
-        inverse = inverse * (2.0 - rho * inverse)
         inverse = inverse * (2.0 - rho * inverse)
         u0 = momentum_ref[0, i] * inverse
         u1 = momentum_ref[1, i] * inverse
@@ -232,16 +242,9 @@
         h = gas_gamma * (energy_ref[i] * inverse) - (gas_gamma - 1.0) * k
         for slot, value in enumerate((u0, u1, u2, h, k)):
             coef_ref[slot, i] = value
-        ahead = tuple(ahead[c] * root + before[c] * (gain * root) for c in range(fields))
-        for c in range(fields):
-            stream_ref[c, i] = ahead[c] - before[c] * edge - stream_ref[c, i]
-        return ahead, tuple(costate_ref[c, i] for c in range(fields))
-
-    before = tuple(even_x_ref[c, 1] * from_left for c in range(fields))
-    ahead = tuple(
-        (even_x_ref[c, 0] * (from_left / root) - before[c]) * gain for c in range(fields)
-    )
-    lax.fori_loop(0, rows, forward, (ahead, before), unroll=4)
+        return carry
+
+    lax.fori_loop(0, rows, state, 0, unroll=8)
 
 
 def early_slope_kernel(rows, *refs):
@@ -291,7 +294,7 @@
             partial_ref[c, i] = costate_ref[c, i] + pulled[c]
         return carry
 
-    lax.fori_loop(0, rows, add, 0, unroll=4)
+    lax.fori_loop(0, rows, add, 0, unroll=8)
 
 
 def pull_stream(a, u0, u1, u2, h, k):

time: 18.7 us -> 17.8 us (0.952)
  Pallas kernels: 9.61 us -> 8.55 us
  starting transfers between devices: 7.66 us -> 8.57 us
  waiting for transfers between devices: 1.24 us -> 0.48 us
    pallas_call x1, Pallas kernels: 3.46 us -> 2.55 us  [per_device(): pl.pallas_call(lambda *refs: early_slope_kernel(rows, *refs), out_shape=(...]
    ppermute x4, starting transfers between devices: 7.66 us -> 8.57 us  [pairs(): return lax.ppermute(values, axis, links)]
    ppermute x4, waiting for transfers between devices: 1.24 us -> 0.48 us  [pairs(): return lax.ppermute(values, axis, links)]
  transfers between devices with their start and end apart: 4 -> 4, of which waited for: 1 -> 1; matrix products, arithmetic and copies ran while one was open for 0% -> 0% of each run, Pallas kernels for 29% -> 24%
where the time goes in v4:
time: 17.8 us; the launch traced here: 17.7 us
  starting transfers between devices  8.57 us (48%)
  Pallas kernels  8.55 us (48%)
  waiting for transfers between devices  0.48 us (3%)
    ppermute x4, starting transfers between devices, pairs(): return lax.ppermute(values, axis, links)  8.57 us
    pallas_call x1, Pallas kernels, per_device(): pl.pallas_call(lambda *refs: early_slope_kernel(rows, *refs), out_shape=(...  2.55 us
    pallas_call x1, Pallas kernels, per_device(): pl.pallas_call(lambda *refs: ends_kernel(rows, *refs), out_shape=(jax.Sha...  2.44 us
    pallas_call x1, Pallas kernels, per_device(): pl.pallas_call(lambda *refs: join_kernel(rows, *refs), out_shape=block, i...  1.86 us
    pallas_call x1, Pallas kernels, per_device(): pl.pallas_call(lambda *refs: gather_kernel(rows, *refs), out_shape=block,...  1.67 us
    ppermute x4, waiting for transfers between devices, pairs(): return lax.ppermute(values, axis, links)  0.48 us
  transfers between devices with their start and end apart: 4, of which 1 were waited for; matrix products, arithmetic and copies ran while one was open for 0% of the time, Pallas kernels for 24%

profile of v4, /device:TPU:8, one launch (start us, length us, event | category | flops | bytes accessed | tf_op | source)
XLA Modules:
  0.0 17.7 jit_solution(7232979211847219634)
XLA Ops:
  0.0 2.4 %ends.1 = (f32[5,8,16,8,128]{4,3,2,1,0:T(8,128)S(1)}, f32[5,2,8,128]{3,2,1,0:T(8,128)S(1)}, f32[5,2,1024]{2,1,0:T(2,128)S(1)}, f32[5,2,1024]{2,1,0:T(2,128)S(1)}...) custom-call(f32[5,8,16,8,128]{4,3,2,1,0:T(8,128)} %bitcast.5, ...), custom_call_target="tpu_custom_call" | custom-call | tf_op jit(solution)/shard_map/ends/pallas_call | solution.py:364
  2.4 0.1 collective-permute-start
  2.5 1.6 %collective-permute-start.1 = (f32[5,2,1024]{2,1,0:T(2,128)S(1)}, f32[5,2,1024]{2,1,0:T(2,128)S(1)}, u32[]{:S(2)}, u32[]{:S(2)}) collective-permute-start(f32[5,2,1024]{2,1,0:T(2,128)S(1)} %get-tuple-element.29), channel_id=1, source_target_pairs={{0,1},{1,0},{2,3},{3,2},{4,5},{5,4},{6,7},{7,6},{8,9},{9,8},{10,11... | collective-permute-start | bytes 122888 | tf_op jit(solution)/shard_map/ppermute | solution.py:397
  4.1 2.0 %collective-permute-start.2 = (f32[5,2,1024]{2,1,0:T(2,128)S(1)}, f32[5,2,1024]{2,1,0:T(2,128)S(1)}, u32[]{:S(2)}, u32[]{:S(2)}) collective-permute-start(f32[5,2,1024]{2,1,0:T(2,128)S(1)} %get-tuple-element.30), channel_id=1, source_target_pairs={{1,2},{2,1},{3,4},{4,3},{5,6},{6,5},{7,0},{0,7},{9,10},{10,9},{11,... | collective-permute-start | bytes 122888 | tf_op jit(solution)/shard_map/ppermute | solution.py:397
  6.1 0.0 collective-permute-done.refs_1_
  6.1 2.6 %early_slope.1 = (f32[5,128,8,128]{3,2,1,0:T(8,128)S(1)}, f32[5,128,8,128]{3,2,1,0:T(8,128)S(1)}, f32[5,128,8,128]{3,2,1,0:T(8,128)S(1)}, f32[5,2,8,128]{3,2,1,0:T(8,128)S(1)}) custom-call(f32[5,128,8,128]{3,2,1,0:T(8,128)S(1)} %bitcast.2, f32[5,2,8,128]{3,2,1,0:T(8,128)S(1)} %collective-permute-done.refs_1_, ...), custom_call_target="tpu_custom_call", output_to_operand_aliasing={{3}: (6, {})} | custom-call | tf_op jit(solution)/shard_map/early_slope/pallas_call | solution.py:409
  8.7 4.9 %collective-permute-start.3 = (f32[5,2,8,128]{3,2,1,0:T(8,128)S(1)}, f32[5,2,8,128]{3,2,1,0:T(8,128)S(1)}, u32[]{:S(2)}, u32[]{:S(2)}) collective-permute-start(f32[5,2,8,128]{3,2,1,0:T(8,128)S(1)} %get-tuple-element.32), channel_id=1, source_target_pairs={{8,16},{16,8},{24,32},{32,24},{40,48},{48,40},{56,64},{64,56},{72,... | collective-permute-start | bytes 122888 | tf_op jit(solution)/shard_map/ppermute | solution.py:397
  13.6 0.0 collective-permute-done.1.refs_4_
  13.6 0.0 collective-permute-done.2.refs_5_
  13.6 1.7 %gather.1.refs_0_ = f32[5,128,8,128]{3,2,1,0:T(8,128)S(1)} custom-call(f32[5,128,8,128]{3,2,1,0:T(8,128)S(1)} %bitcast.4, f32[5,128,8,128]{3,2,1,0:T(8,128)S(1)} %get-tuple-element.26.refs_1_, f32[5,128,8,128]{3,2,1,0:T(8,128)S(1)} %get-tuple-element.27.refs_2_, f32[5,128,8,128]{3,2,1,0:T(8,128)S(1)} %get-tuple-element.28.refs_3_.refs_1_, ...), custom_call_target="tpu_custom_call" | custom-call | flops 100000000 | bytes 10000000 | tf_op jit(solution)/shard_map/gather/pallas_call | solution.py:434
  15.3 0.5 %collective-permute-done.3.refs_2_ = f32[5,2,8,128]{3,2,1,0:T(8,128)S(1)} collective-permute-done((f32[5,2,8,128]{3,2,1,0:T(8,128)S(1)}, f32[5,2,8,128]{3,2,1,0:T(8,128)S(1)}, u32[]{:S(2)}, u32[]{:S(2)}) %collective-permute-start.3) | collective-permute-done | bytes 40992 | tf_op jit(solution)/shard_map/ppermute | solution.py:397
  15.8 1.9 %join.1 = f32[5,128,8,128]{3,2,1,0:T(8,128)} custom-call(f32[5,128,8,128]{3,2,1,0:T(8,128)S(1)} %gather.1.refs_0_, f32[5,128,8,128]{3,2,1,0:T(8,128)S(1)} %get-tuple-element.28.refs_3_.refs_1_, f32[5,2,8,128]{3,2,1,0:T(8,128)S(1)} %collective-permute-done.3.refs_2_), custom_call_target="tpu_custom_call" | custom-call | tf_op jit(solution)/shard_map/join/pallas_call | solution.py:448
  (1 shorter events, 0.0 us)
Async XLA Ops:
  2.4 3.7 %collective-permute-start = (f32[5,2,8,128]{3,2,1,0:T(8,128)S(1)}, f32[5,2,8,128]{3,2,1,0:T(8,128)S(1)}, u32[]{:S(2)}, u32[]{:S(2)}) collective-permute-start(f32[5,2,8,128]{3,2,1,0:T(8,128)S(1)} %get-tuple-element.20), channel_id=1, source_target_pairs={{0,8},{8,0},{16,24},{24,16},{32,40},{40,32},{48,56},{56,48},{64,72... | collective-permute-start | bytes 122888 | tf_op jit(solution)/shard_map/ppermute | solution.py:397
  2.5 11.1 %collective-permute-start.1 = (f32[5,2,1024]{2,1,0:T(2,128)S(1)}, f32[5,2,1024]{2,1,0:T(2,128)S(1)}, u32[]{:S(2)}, u32[]{:S(2)}) collective-permute-start(f32[5,2,1024]{2,1,0:T(2,128)S(1)} %get-tuple-element.29), channel_id=1, source_target_pairs={{0,1},{1,0},{2,3},{3,2},{4,5},{5,4},{6,7},{7,6},{8,9},{9,8},{10,11... | collective-permute-start | bytes 122888 | tf_op jit(solution)/shard_map/ppermute | solution.py:397
  4.1 9.5 %collective-permute-start.2 = (f32[5,2,1024]{2,1,0:T(2,128)S(1)}, f32[5,2,1024]{2,1,0:T(2,128)S(1)}, u32[]{:S(2)}, u32[]{:S(2)}) collective-permute-start(f32[5,2,1024]{2,1,0:T(2,128)S(1)} %get-tuple-element.30), channel_id=1, source_target_pairs={{1,2},{2,1},{3,4},{4,3},{5,6},{6,5},{7,0},{0,7},{9,10},{10,9},{11,... | collective-permute-start | bytes 122888 | tf_op jit(solution)/shard_map/ppermute | solution.py:397
  8.7 7.1 %collective-permute-start.3 = (f32[5,2,8,128]{3,2,1,0:T(8,128)S(1)}, f32[5,2,8,128]{3,2,1,0:T(8,128)S(1)}, u32[]{:S(2)}, u32[]{:S(2)}) collective-permute-start(f32[5,2,8,128]{3,2,1,0:T(8,128)S(1)} %get-tuple-element.32), channel_id=1, source_target_pairs={{8,16},{16,8},{24,32},{32,24},{40,48},{48,40},{56,64},{64,56},{72,... | collective-permute-start | bytes 122888 | tf_op jit(solution)/shard_map/ppermute | solution.py:397

commit v5 on v4

--- a/solution.py
+++ b/solution.py
@@ -21,6 +21,7 @@
 
 fields = 5
 segments = 8
+pieces = 16
 arrival_depth = 24
 vmem_bytes = 16 * 1024 * 1024
 
@@ -244,7 +245,7 @@
             coef_ref[slot, i] = value
         return carry
 
-    lax.fori_loop(0, rows, state, 0, unroll=8)
+    lax.fori_loop(0, rows, state, 0, unroll=16)
 
 
 def early_slope_kernel(rows, *refs):
@@ -294,7 +295,7 @@
             partial_ref[c, i] = costate_ref[c, i] + pulled[c]
         return carry
 
-    lax.fori_loop(0, rows, add, 0, unroll=8)
+    lax.fori_loop(0, rows, add, 0, unroll=16)
 
 
 def pull_stream(a, u0, u1, u2, h, k):
@@ -313,11 +314,11 @@
 
 def join_kernel(rows, partial_ref, coef_ref, odd_x_ref, out_hbm, result, sems):
     place = lax.axis_index("gx") % 2
-    per_segment = rows // segments
+    per_segment = rows // pieces
     sign = jnp.where(place == 0, 1.0, -1.0).astype(jnp.float32)
 
     def copy_out(s):
-        at = jnp.where(place == 0, s, segments - 1 - s)
+        at = jnp.where(place == 0, s, pieces - 1 - s)
         part = pl.ds(at * per_segment, per_segment)
         return pltpu.make_async_copy(result.at[:, part], out_hbm.at[:, part], sems.at[s])
 
@@ -339,13 +340,13 @@
         return carry
 
     total = tuple(odd_x_ref[c, 0] * (sign * (step_scale * tail)) for c in range(fields))
-    lax.fori_loop(0, segments, segment, total)
+    lax.fori_loop(0, pieces, segment, total)
 
     def finish(s, carry):
         copy_out(s).wait()
         return carry
 
-    lax.fori_loop(0, segments, finish, 0)
+    lax.fori_loop(0, pieces, finish, 0)
 
 
 def per_device(density, momentum, energy, costate):
@@ -452,7 +453,7 @@
         out_specs=hbm,
         scratch_shapes=[
             pltpu.VMEM((fields, rows, planes, cells), f32),
-            pltpu.SemaphoreType.DMA((segments,)),
+            pltpu.SemaphoreType.DMA((pieces,)),
         ],
         compiler_params=params,
         name="join",

time: 17.8 us -> 17.6 us (0.989)
  Pallas kernels: 8.55 us -> 8.27 us
where the time goes in v5:
time: 17.6 us; the launch traced here: 17.4 us
  starting transfers between devices  8.65 us (49%)
  Pallas kernels  8.27 us (47%)
  waiting for transfers between devices  0.47 us (3%)
    ppermute x4, starting transfers between devices, pairs(): return lax.ppermute(values, axis, links)  8.65 us
    pallas_call x1, Pallas kernels, per_device(): pl.pallas_call(lambda *refs: early_slope_kernel(rows, *refs), out_shape=(...  2.47 us
    pallas_call x1, Pallas kernels, per_device(): pl.pallas_call(lambda *refs: ends_kernel(rows, *refs), out_shape=(jax.Sha...  2.44 us
    pallas_call x1, Pallas kernels, per_device(): pl.pallas_call(lambda *refs: join_kernel(rows, *refs), out_shape=block, i...  1.72 us
    pallas_call x1, Pallas kernels, per_device(): pl.pallas_call(lambda *refs: gather_kernel(rows, *refs), out_shape=block,...  1.61 us
    ppermute x4, waiting for transfers between devices, pairs(): return lax.ppermute(values, axis, links)  0.47 us
  transfers between devices with their start and end apart: 4, of which 1 were waited for; matrix products, arithmetic and copies ran while one was open for 0% of the time, Pallas kernels for 24%

profile of v5, /device:TPU:8, one launch (start us, length us, event | category | flops | bytes accessed | tf_op | source)
XLA Modules:
  0.0 17.4 jit_solution(13543445543668758847)
XLA Ops:
  0.0 2.4 %ends.1 = (f32[5,8,16,8,128]{4,3,2,1,0:T(8,128)S(1)}, f32[5,2,8,128]{3,2,1,0:T(8,128)S(1)}, f32[5,2,1024]{2,1,0:T(2,128)S(1)}, f32[5,2,1024]{2,1,0:T(2,128)S(1)}...) custom-call(f32[5,8,16,8,128]{4,3,2,1,0:T(8,128)} %bitcast.5, ...), custom_call_target="tpu_custom_call" | custom-call | tf_op jit(solution)/shard_map/ends/pallas_call | solution.py:365
  2.4 0.1 collective-permute-start
  2.5 1.6 %collective-permute-start.1 = (f32[5,2,1024]{2,1,0:T(2,128)S(1)}, f32[5,2,1024]{2,1,0:T(2,128)S(1)}, u32[]{:S(2)}, u32[]{:S(2)}) collective-permute-start(f32[5,2,1024]{2,1,0:T(2,128)S(1)} %get-tuple-element.29), channel_id=1, source_target_pairs={{0,1},{1,0},{2,3},{3,2},{4,5},{5,4},{6,7},{7,6},{8,9},{9,8},{10,11... | collective-permute-start | bytes 122888 | tf_op jit(solution)/shard_map/ppermute | solution.py:398
  4.1 2.0 %collective-permute-start.2 = (f32[5,2,1024]{2,1,0:T(2,128)S(1)}, f32[5,2,1024]{2,1,0:T(2,128)S(1)}, u32[]{:S(2)}, u32[]{:S(2)}) collective-permute-start(f32[5,2,1024]{2,1,0:T(2,128)S(1)} %get-tuple-element.30), channel_id=1, source_target_pairs={{1,2},{2,1},{3,4},{4,3},{5,6},{6,5},{7,0},{0,7},{9,10},{10,9},{11,... | collective-permute-start | bytes 122888 | tf_op jit(solution)/shard_map/ppermute | solution.py:398
  6.1 0.0 collective-permute-done.refs_1_
  6.1 2.5 %early_slope.1 = (f32[5,128,8,128]{3,2,1,0:T(8,128)S(1)}, f32[5,128,8,128]{3,2,1,0:T(8,128)S(1)}, f32[5,128,8,128]{3,2,1,0:T(8,128)S(1)}, f32[5,2,8,128]{3,2,1,0:T(8,128)S(1)}) custom-call(f32[5,128,8,128]{3,2,1,0:T(8,128)S(1)} %bitcast.2, f32[5,2,8,128]{3,2,1,0:T(8,128)S(1)} %collective-permute-done.refs_1_, ...), custom_call_target="tpu_custom_call", output_to_operand_aliasing={{3}: (6, {})} | custom-call | tf_op jit(solution)/shard_map/early_slope/pallas_call | solution.py:410
  8.6 5.0 %collective-permute-start.3 = (f32[5,2,8,128]{3,2,1,0:T(8,128)S(1)}, f32[5,2,8,128]{3,2,1,0:T(8,128)S(1)}, u32[]{:S(2)}, u32[]{:S(2)}) collective-permute-start(f32[5,2,8,128]{3,2,1,0:T(8,128)S(1)} %get-tuple-element.32), channel_id=1, source_target_pairs={{8,16},{16,8},{24,32},{32,24},{40,48},{48,40},{56,64},{64,56},{72,... | collective-permute-start | bytes 122888 | tf_op jit(solution)/shard_map/ppermute | solution.py:398
  13.6 0.0 collective-permute-done.1.refs_4_
  13.6 0.0 collective-permute-done.2.refs_5_
  13.6 1.6 %gather.1.refs_0_ = f32[5,128,8,128]{3,2,1,0:T(8,128)S(1)} custom-call(f32[5,128,8,128]{3,2,1,0:T(8,128)S(1)} %bitcast.4, f32[5,128,8,128]{3,2,1,0:T(8,128)S(1)} %get-tuple-element.26.refs_1_, f32[5,128,8,128]{3,2,1,0:T(8,128)S(1)} %get-tuple-element.27.refs_2_, f32[5,128,8,128]{3,2,1,0:T(8,128)S(1)} %get-tuple-element.28.refs_3_.refs_1_, ...), custom_call_target="tpu_custom_call" | custom-call | flops 100000000 | bytes 10000000 | tf_op jit(solution)/shard_map/gather/pallas_call | solution.py:435
  15.3 0.5 %collective-permute-done.3.refs_2_ = f32[5,2,8,128]{3,2,1,0:T(8,128)S(1)} collective-permute-done((f32[5,2,8,128]{3,2,1,0:T(8,128)S(1)}, f32[5,2,8,128]{3,2,1,0:T(8,128)S(1)}, u32[]{:S(2)}, u32[]{:S(2)}) %collective-permute-start.3) | collective-permute-done | bytes 40992 | tf_op jit(solution)/shard_map/ppermute | solution.py:398
  15.7 1.7 %join.1 = f32[5,128,8,128]{3,2,1,0:T(8,128)} custom-call(f32[5,128,8,128]{3,2,1,0:T(8,128)S(1)} %gather.1.refs_0_, f32[5,128,8,128]{3,2,1,0:T(8,128)S(1)} %get-tuple-element.28.refs_3_.refs_1_, f32[5,2,8,128]{3,2,1,0:T(8,128)S(1)} %collective-permute-done.3.refs_2_), custom_call_target="tpu_custom_call" | custom-call | tf_op jit(solution)/shard_map/join/pallas_call | solution.py:449
  (1 shorter events, 0.0 us)
Async XLA Ops:
  2.4 3.7 %collective-permute-start = (f32[5,2,8,128]{3,2,1,0:T(8,128)S(1)}, f32[5,2,8,128]{3,2,1,0:T(8,128)S(1)}, u32[]{:S(2)}, u32[]{:S(2)}) collective-permute-start(f32[5,2,8,128]{3,2,1,0:T(8,128)S(1)} %get-tuple-element.20), channel_id=1, source_target_pairs={{0,8},{8,0},{16,24},{24,16},{32,40},{40,32},{48,56},{56,48},{64,72... | collective-permute-start | bytes 122888 | tf_op jit(solution)/shard_map/ppermute | solution.py:398
  2.5 11.1 %collective-permute-start.1 = (f32[5,2,1024]{2,1,0:T(2,128)S(1)}, f32[5,2,1024]{2,1,0:T(2,128)S(1)}, u32[]{:S(2)}, u32[]{:S(2)}) collective-permute-start(f32[5,2,1024]{2,1,0:T(2,128)S(1)} %get-tuple-element.29), channel_id=1, source_target_pairs={{0,1},{1,0},{2,3},{3,2},{4,5},{5,4},{6,7},{7,6},{8,9},{9,8},{10,11... | collective-permute-start | bytes 122888 | tf_op jit(solution)/shard_map/ppermute | solution.py:398
  4.1 9.5 %collective-permute-start.2 = (f32[5,2,1024]{2,1,0:T(2,128)S(1)}, f32[5,2,1024]{2,1,0:T(2,128)S(1)}, u32[]{:S(2)}, u32[]{:S(2)}) collective-permute-start(f32[5,2,1024]{2,1,0:T(2,128)S(1)} %get-tuple-element.30), channel_id=1, source_target_pairs={{1,2},{2,1},{3,4},{4,3},{5,6},{6,5},{7,0},{0,7},{9,10},{10,9},{11,... | collective-permute-start | bytes 122888 | tf_op jit(solution)/shard_map/ppermute | solution.py:398
  8.6 7.1 %collective-permute-start.3 = (f32[5,2,8,128]{3,2,1,0:T(8,128)S(1)}, f32[5,2,8,128]{3,2,1,0:T(8,128)S(1)}, u32[]{:S(2)}, u32[]{:S(2)}) collective-permute-start(f32[5,2,8,128]{3,2,1,0:T(8,128)S(1)} %get-tuple-element.32), channel_id=1, source_target_pairs={{8,16},{16,8},{24,32},{32,24},{40,48},{48,40},{56,64},{64,56},{72,... | collective-permute-start | bytes 122888 | tf_op jit(solution)/shard_map/ppermute | solution.py:398

commit v6 on v5

--- a/solution.py
+++ b/solution.py
@@ -173,16 +173,18 @@
     rows, costate_ref, even_x_ref, matrix_ref, density_hbm, momentum_hbm, energy_hbm,
     stream_ref, span_ref, coef_ref, density_ref, momentum_ref, energy_ref, sems,
 ):
-    copies = [
-        pltpu.make_async_copy(source, target, sems.at[n])
+    half = rows // 2
+    copies = []
+    for part in range(2):
+        at = pl.ds(part * half, half)
         for n, (source, target) in enumerate(
             (
-                (density_hbm, density_ref),
-                (momentum_hbm, momentum_ref),
-                (energy_hbm, energy_ref),
+                (density_hbm.at[at], density_ref.at[at]),
+                (momentum_hbm.at[:, at], momentum_ref.at[:, at]),
+                (energy_hbm.at[at], energy_ref.at[at]),
             )
-        )
-    ]
+        ):
+            copies.append(pltpu.make_async_copy(source, target, sems.at[3 * part + n]))
     for copy in copies:
         copy.start()
     x_even = lax.axis_index("gx") % 2 == 0
@@ -229,8 +231,6 @@
         (even_x_ref[c, 0] * (from_left / root) - before[c]) * gain for c in range(fields)
     )
     lax.fori_loop(0, rows, forward, (ahead, before), unroll=8)
-    for copy in copies:
-        copy.wait()
 
     def state(i, carry):
         rho = density_ref[i]
@@ -245,7 +245,10 @@
             coef_ref[slot, i] = value
         return carry
 
-    lax.fori_loop(0, rows, state, 0, unroll=16)
+    for part in range(2):
+        for copy in copies[3 * part : 3 * part + 3]:
+            copy.wait()
+        lax.fori_loop(part * half, (part + 1) * half, state, 0, unroll=8)
 
 
 def early_slope_kernel(rows, *refs):
@@ -412,7 +415,7 @@
         out_shape=(block, block, block, x_shape),
         in_specs=[whole] * 3 + [hbm] * 3 + [whole],
         out_specs=(whole,) * 4,
-        scratch_shapes=[*state, pltpu.SemaphoreType.DMA((3,))],
+        scratch_shapes=[*state, pltpu.SemaphoreType.DMA((6,))],
         input_output_aliases={6: 3},
         compiler_params=params,
         name="early_slope",
@@ -425,7 +428,7 @@
         out_shape=(block,) * 3,
         in_specs=[whole] * 3 + [hbm] * 3 + [whole] * 3,
         out_specs=(whole,) * 3,
-        scratch_shapes=[*state, pltpu.SemaphoreType.DMA((3,))],
+        scratch_shapes=[*state, pltpu.SemaphoreType.DMA((6,))],
         input_output_aliases={6: 0, 7: 1, 8: 2},
         compiler_params=params,
         cost_estimate=pl.CostEstimate(flops=300_000_000, bytes_accessed=10_000_000, transcendentals=0),

time: 17.6 us -> 17.7 us (level)
  no operation moved by 1% of the time
where the time goes in v6:
time: 17.7 us; the launch traced here: 17.6 us
  starting transfers between devices  8.56 us (48%)
  Pallas kernels  8.41 us (48%)
  waiting for transfers between devices  0.53 us (3%)
    ppermute x4, starting transfers between devices, pairs(): return lax.ppermute(values, axis, links)  8.56 us
    pallas_call x1, Pallas kernels, per_device(): pl.pallas_call(lambda *refs: early_slope_kernel(rows, *refs), out_shape=(...  2.59 us
    pallas_call x1, Pallas kernels, per_device(): pl.pallas_call(lambda *refs: ends_kernel(rows, *refs), out_shape=(jax.Sha...  2.44 us
    pallas_call x1, Pallas kernels, per_device(): pl.pallas_call(lambda *refs: join_kernel(rows, *refs), out_shape=block, i...  1.72 us
    pallas_call x1, Pallas kernels, per_device(): pl.pallas_call(lambda *refs: gather_kernel(rows, *refs), out_shape=block,...  1.61 us
    ppermute x4, waiting for transfers between devices, pairs(): return lax.ppermute(values, axis, links)  0.53 us
  transfers between devices with their start and end apart: 4, of which 1 were waited for; matrix products, arithmetic and copies ran while one was open for 0% of the time, Pallas kernels for 24%

profile of v6, /device:TPU:8, one launch (start us, length us, event | category | flops | bytes accessed | tf_op | source)
XLA Modules:
  0.0 17.6 jit_solution(13474853191980566302)
XLA Ops:
  0.0 2.4 %ends.1 = (f32[5,8,16,8,128]{4,3,2,1,0:T(8,128)S(1)}, f32[5,2,8,128]{3,2,1,0:T(8,128)S(1)}, f32[5,2,1024]{2,1,0:T(2,128)S(1)}, f32[5,2,1024]{2,1,0:T(2,128)S(1)}...) custom-call(f32[5,8,16,8,128]{4,3,2,1,0:T(8,128)} %bitcast.5, ...), custom_call_target="tpu_custom_call" | custom-call | tf_op jit(solution)/shard_map/ends/pallas_call | solution.py:368
  2.4 0.1 collective-permute-start
  2.5 1.6 %collective-permute-start.1 = (f32[5,2,1024]{2,1,0:T(2,128)S(1)}, f32[5,2,1024]{2,1,0:T(2,128)S(1)}, u32[]{:S(2)}, u32[]{:S(2)}) collective-permute-start(f32[5,2,1024]{2,1,0:T(2,128)S(1)} %get-tuple-element.29), channel_id=1, source_target_pairs={{0,1},{1,0},{2,3},{3,2},{4,5},{5,4},{6,7},{7,6},{8,9},{9,8},{10,11... | collective-permute-start | bytes 122888 | tf_op jit(solution)/shard_map/ppermute | solution.py:401
  4.1 2.0 %collective-permute-start.2 = (f32[5,2,1024]{2,1,0:T(2,128)S(1)}, f32[5,2,1024]{2,1,0:T(2,128)S(1)}, u32[]{:S(2)}, u32[]{:S(2)}) collective-permute-start(f32[5,2,1024]{2,1,0:T(2,128)S(1)} %get-tuple-element.30), channel_id=1, source_target_pairs={{1,2},{2,1},{3,4},{4,3},{5,6},{6,5},{7,0},{0,7},{9,10},{10,9},{11,... | collective-permute-start | bytes 122888 | tf_op jit(solution)/shard_map/ppermute | solution.py:401
  6.1 0.0 collective-permute-done.refs_1_
  6.1 2.6 %early_slope.1 = (f32[5,128,8,128]{3,2,1,0:T(8,128)S(1)}, f32[5,128,8,128]{3,2,1,0:T(8,128)S(1)}, f32[5,128,8,128]{3,2,1,0:T(8,128)S(1)}, f32[5,2,8,128]{3,2,1,0:T(8,128)S(1)}) custom-call(f32[5,128,8,128]{3,2,1,0:T(8,128)S(1)} %bitcast.2, f32[5,2,8,128]{3,2,1,0:T(8,128)S(1)} %collective-permute-done.refs_1_, ...), custom_call_target="tpu_custom_call", output_to_operand_aliasing={{3}: (6, {})} | custom-call | tf_op jit(solution)/shard_map/early_slope/pallas_call | solution.py:413
  8.7 4.9 %collective-permute-start.3 = (f32[5,2,8,128]{3,2,1,0:T(8,128)S(1)}, f32[5,2,8,128]{3,2,1,0:T(8,128)S(1)}, u32[]{:S(2)}, u32[]{:S(2)}) collective-permute-start(f32[5,2,8,128]{3,2,1,0:T(8,128)S(1)} %get-tuple-element.32), channel_id=1, source_target_pairs={{8,16},{16,8},{24,32},{32,24},{40,48},{48,40},{56,64},{64,56},{72,... | collective-permute-start | bytes 122888 | tf_op jit(solution)/shard_map/ppermute | solution.py:401
  13.6 0.1 late_slope.1
  13.7 0.0 collective-permute-done.1.refs_4_
  13.7 0.0 collective-permute-done.2.refs_5_
  13.7 1.6 %gather.1.refs_0_ = f32[5,128,8,128]{3,2,1,0:T(8,128)S(1)} custom-call(f32[5,128,8,128]{3,2,1,0:T(8,128)S(1)} %bitcast.4, f32[5,128,8,128]{3,2,1,0:T(8,128)S(1)} %get-tuple-element.26.refs_1_, f32[5,128,8,128]{3,2,1,0:T(8,128)S(1)} %get-tuple-element.27.refs_2_, f32[5,128,8,128]{3,2,1,0:T(8,128)S(1)} %get-tuple-element.28.refs_3_.refs_1_, ...), custom_call_target="tpu_custom_call" | custom-call | flops 100000000 | bytes 10000000 | tf_op jit(solution)/shard_map/gather/pallas_call | solution.py:438
  15.3 0.5 %collective-permute-done.3.refs_2_ = f32[5,2,8,128]{3,2,1,0:T(8,128)S(1)} collective-permute-done((f32[5,2,8,128]{3,2,1,0:T(8,128)S(1)}, f32[5,2,8,128]{3,2,1,0:T(8,128)S(1)}, u32[]{:S(2)}, u32[]{:S(2)}) %collective-permute-start.3) | collective-permute-done | bytes 40992 | tf_op jit(solution)/shard_map/ppermute | solution.py:401
  15.8 1.7 %join.1 = f32[5,128,8,128]{3,2,1,0:T(8,128)} custom-call(f32[5,128,8,128]{3,2,1,0:T(8,128)S(1)} %gather.1.refs_0_, f32[5,128,8,128]{3,2,1,0:T(8,128)S(1)} %get-tuple-element.28.refs_3_.refs_1_, f32[5,2,8,128]{3,2,1,0:T(8,128)S(1)} %collective-permute-done.3.refs_2_), custom_call_target="tpu_custom_call" | custom-call | tf_op jit(solution)/shard_map/join/pallas_call | solution.py:452
Async XLA Ops:
  2.4 3.7 %collective-permute-start = (f32[5,2,8,128]{3,2,1,0:T(8,128)S(1)}, f32[5,2,8,128]{3,2,1,0:T(8,128)S(1)}, u32[]{:S(2)}, u32[]{:S(2)}) collective-permute-start(f32[5,2,8,128]{3,2,1,0:T(8,128)S(1)} %get-tuple-element.20), channel_id=1, source_target_pairs={{0,8},{8,0},{16,24},{24,16},{32,40},{40,32},{48,56},{56,48},{64,72... | collective-permute-start | bytes 122888 | tf_op jit(solution)/shard_map/ppermute | solution.py:401
  2.5 11.1 %collective-permute-start.1 = (f32[5,2,1024]{2,1,0:T(2,128)S(1)}, f32[5,2,1024]{2,1,0:T(2,128)S(1)}, u32[]{:S(2)}, u32[]{:S(2)}) collective-permute-start(f32[5,2,1024]{2,1,0:T(2,128)S(1)} %get-tuple-element.29), channel_id=1, source_target_pairs={{0,1},{1,0},{2,3},{3,2},{4,5},{5,4},{6,7},{7,6},{8,9},{9,8},{10,11... | collective-permute-start | bytes 122888 | tf_op jit(solution)/shard_map/ppermute | solution.py:401
  4.1 9.6 %collective-permute-start.2 = (f32[5,2,1024]{2,1,0:T(2,128)S(1)}, f32[5,2,1024]{2,1,0:T(2,128)S(1)}, u32[]{:S(2)}, u32[]{:S(2)}) collective-permute-start(f32[5,2,1024]{2,1,0:T(2,128)S(1)} %get-tuple-element.30), channel_id=1, source_target_pairs={{1,2},{2,1},{3,4},{4,3},{5,6},{6,5},{7,0},{0,7},{9,10},{10,9},{11,... | collective-permute-start | bytes 122888 | tf_op jit(solution)/shard_map/ppermute | solution.py:401
  8.7 7.1 %collective-permute-start.3 = (f32[5,2,8,128]{3,2,1,0:T(8,128)S(1)}, f32[5,2,8,128]{3,2,1,0:T(8,128)S(1)}, u32[]{:S(2)}, u32[]{:S(2)}) collective-permute-start(f32[5,2,8,128]{3,2,1,0:T(8,128)S(1)} %get-tuple-element.32), channel_id=1, source_target_pairs={{8,16},{16,8},{24,32},{32,24},{40,48},{48,40},{56,64},{64,56},{72,... | collective-permute-start | bytes 122888 | tf_op jit(solution)/shard_map/ppermute | solution.py:401
